TPU v7x, 256 devices: a whole 4x4x8 slice. The times are simulated.
256 devices in a mesh: group: 8 (over z), prefix: 32 (over x, y, core).
Axes of the slice: x: 4, y: 4, z: 8, core: 2. Of those that a mesh axis runs over, the one named last changes fastest.
Arguments:
- queries: bfloat16 [4096, 64, 128], P('prefix', 'group'), may hold values from -41 to 41
- prefix_keys: bfloat16 [4096, 8, 128], P(('group', 'prefix')), may hold values from -5 to 5
- prefix_values: bfloat16 [4096, 8, 128], P(('group', 'prefix')), may hold values from -24 to 24
- out_grad: bfloat16 [4096, 64, 128], P('prefix', 'group'), may hold values from -6 to 6
- tile_mask: int32 [2, 32], replicated, may hold values 0 or 1
- lengths: int32 [2], replicated, may hold values from 1024 to 2048, as said below
Outputs:
- attended: bfloat16 [4096, 64, 128], P('prefix', 'group')
- query_grad: bfloat16 [4096, 64, 128], P('prefix', 'group')
- key_grad: float32 [4096, 8, 128], P(('group', 'prefix'))
- value_grad: float32 [4096, 8, 128], P(('group', 'prefix'))
Inputs may be any that keep to these rules, and one draw needn't show every extreme that they name: `tile_mask`: a 0 or 1 flag for each completion and prompt tile. `lengths`: one completion has exactly 2048 tokens.
All inputs are finite; a program needn't handle non-finite values.
Results may differ from a plain program's by a relative error of at most 0.035.
Values may be sent and summed in bfloat16 or wider, within the bound.
A program may use at most 128 MiB of HBM per device.

v0:
```python
import math

import jax
import jax.numpy as jnp
from jax import lax
from jax.sharding import PartitionSpec as P

PTILE = 128


big_negative = -1e30


def on_device(queries, prefix_keys, prefix_values, out_grad, tile_mask, lengths):
    parts_count = lax.axis_size("prefix")
    teams_count = lax.axis_size("group")
    my_part = lax.axis_index("prefix")
    tok_rows, head_count, head_size = queries.shape
    shard_rows = prefix_keys.shape[0]
    kv_local = prefix_keys.shape[1] // teams_count
    per_group = head_count // kv_local
    inv_root = 1.0 / math.sqrt(head_size)
    span_len = min(2048, tok_rows * parts_count // 2)
    first_tok = my_part * tok_rows
    which_comp = first_tok // span_len
    tok_index = first_tok + jnp.arange(tok_rows, dtype=jnp.int32)
    allowed = lax.dynamic_index_in_dim(lengths, which_comp, 0, keepdims=False)
    is_valid = tok_index % span_len < allowed
    mask_row = lax.dynamic_index_in_dim(tile_mask, which_comp, 0, keepdims=False)
    tile_ids = jnp.arange(mask_row.shape[0], dtype=jnp.int32)
    query_four = queries.reshape(tok_rows, kv_local, per_group, head_size)
    grad_keep = jnp.where(is_valid[:, None, None], out_grad, jnp.zeros_like(out_grad))
    grad_four = grad_keep.reshape(tok_rows, kv_local, per_group, head_size)
    valid_four = is_valid.astype(jnp.float32)[:, None, None, None]
    owned_keys, owned_values = (
        lax.all_to_all(prefix_keys, "group", split_axis=1, concat_axis=0, tiled=True),
        lax.all_to_all(prefix_values, "group", split_axis=1, concat_axis=0, tiled=True),
    )
    all_keys, all_values = (
        lax.all_gather(owned_keys, "prefix", axis=0, tiled=True),
        lax.all_gather(owned_values, "prefix", axis=0, tiled=True),
    )
    order_idx = jnp.arange(all_keys.shape[0], dtype=jnp.int32)
    src_part = order_idx // (teams_count * shard_rows)
    src_team = order_idx // shard_rows % teams_count
    tiles = ((src_team * parts_count + src_part) * shard_rows + order_idx % shard_rows) // PTILE
    hits = (tiles[:, None] == tile_ids[None, :]) & (mask_row[None, :] == 1)
    all_seen = jnp.any(hits, axis=1) | (tiles == 0)
    score = jnp.where(
        all_seen,
        jnp.einsum("tgrd,sgd->gtrs", query_four, all_keys, preferred_element_type=jnp.float32)
        * inv_root,
        big_negative,
    )
    row_top = jnp.max(score, axis=3)
    row_sum = jnp.sum(jnp.where(all_seen, jnp.exp(score - row_top[..., None]), 0.0), axis=3)
    log_total = row_top + jnp.log(row_sum)
    prob = jnp.where(all_seen, jnp.exp(score - log_total[..., None]), 0.0)
    weights = prob.astype(jnp.bfloat16)
    mixed = jnp.einsum("gtrs,sgd->tgrd", weights, all_values, preferred_element_type=jnp.float32)
    mixed = mixed * valid_four
    attended = mixed.astype(jnp.bfloat16).reshape(tok_rows, head_count, head_size)
    offset = jnp.sum(grad_four.astype(jnp.float32) * mixed, axis=3)
    offset_heads = jnp.transpose(offset, (1, 0, 2))[..., None]
    value_dot = jnp.einsum(
        "tgrd,sgd->gtrs", grad_four, all_values, preferred_element_type=jnp.float32
    )
    dscore = (prob * (value_dot - offset_heads)).astype(jnp.bfloat16)
    query_part = (
        jnp.einsum("gtrs,sgd->tgrd", dscore, all_keys, preferred_element_type=jnp.float32)
        * inv_root
    )
    query_grad = query_part.astype(jnp.bfloat16).reshape(tok_rows, head_count, head_size)
    key_part = (
        jnp.einsum("gtrs,tgrd->sgd", dscore, query_four, preferred_element_type=jnp.float32)
        * inv_root
    )
    value_part = jnp.einsum(
        "gtrs,tgrd->sgd", weights, grad_four, preferred_element_type=jnp.float32
    )
    key_sum, value_sum = (
        lax.psum_scatter(
            key_part.astype(jnp.bfloat16), "prefix", scatter_dimension=0, tiled=True
        ).astype(jnp.float32),
        lax.psum_scatter(
            value_part.astype(jnp.bfloat16), "prefix", scatter_dimension=0, tiled=True
        ).astype(jnp.float32),
    )
    key_grad, value_grad = (
        lax.all_to_all(
            key_sum.astype(jnp.bfloat16), "group", split_axis=0, concat_axis=1, tiled=True
        ).astype(key_sum.dtype),
        lax.all_to_all(
            value_sum.astype(jnp.bfloat16), "group", split_axis=0, concat_axis=1, tiled=True
        ).astype(value_sum.dtype),
    )
    return (attended, query_grad, key_grad, value_grad)


def solution(mesh):
    return jax.shard_map(
        on_device,
        mesh=mesh,
        in_specs=(
            P("prefix", "group", None),
            P(("group", "prefix"), None, None),
            P(("group", "prefix"), None, None),
            P("prefix", "group", None),
            P(),
            P(),
        ),
        out_specs=(
            P("prefix", "group", None),
            P("prefix", "group", None),
            P(("group", "prefix"), None, None),
            P(("group", "prefix"), None, None),
        ),
        check_vma=False,
    )
```

profile of v0, /device:TPU:1, one launch (start us, length us, event | category | flops | bytes accessed | tf_op | source)
XLA Modules:
  0.0 341.9 jit_solution(4255468276615843069)
XLA Ops:
  7.2 0.8 copy.52
  8.0 15.8 %all_to_all.54 = bf16[16,8,128]{2,0,1:T(8,128)(2,1)} all-to-all(bf16[16,8,128]{2,0,1:T(8,128)(2,1)S(1)} %copy.52), channel_id=1, replica_groups=mesh['group'=8,'prefix'=32] {'group'}, dimensions={1} | all-to-all | bytes 65536 | tf_op jit(solution)/shard_map/all_to_all | solution.py:36
  23.8 1.4 copy.54
  25.2 3.3 all-to-all-start.1
  28.6 1.2 copy.56
  29.7 1.2 dynamic_slice.9
  31.0 0.7 compare_bitcast_fusion
  31.9 0.7 fusion.44
  32.5 2.8 all-to-all-done.1
  35.3 0.7 copy.55
  36.1 33.8 %all-gather.3.cloned.1.call-done = bf16[4096,1,128]{2,0,1:T(8,128)(2,1)} async-done(((bf16[128,1,128]{2,0,1:T(8,128)(2,1)}), bf16[4096,1,128]{2,0,1:T(8,128)(2,1)}) %all-gather.3.cloned.1.call-update) | async-done | bytes 1048592 | tf_op jit(solution)/shard_map/all_gather | solution.py:40
  69.9 4.2 %fusion.1 = (f32[128,8]{0,1:T(8,128)S(1)}, f32[128,8,4096]{2,0,1:T(8,128)S(1)}) fusion(pred[4096]{0:T(1024)(128)(4,1)S(1)} %compare_or_fusion, bf16[4096,1,128]{2,0,1:T(8,128)(2,1)} %all-gather.3.cloned.1.call-done, bf16[128,8,128]{2,1,0:T(8,128)(2,1)} %param.6), kind=kOutput, calls=%fused_computation.5 | convolution fusion | flops 1086323712 | bytes 18096128 | tf_op jit(solution)/shard_map/tgrd,sgd->gtrs/dot_general | solution.py:51
  74.1 5.7 %copy-done = f32[128,8,4096]{2,0,1:T(8,128)} copy-done((f32[128,8,4096]{2,0,1:T(8,128)}, f32[128,8,4096]{2,0,1:T(8,128)S(1)}, u32[]{:S(2)}) %copy-start) | copy-done | bytes 16777240
  79.9 4.9 %select_reduce_fusion = f32[128,8]{0,1:T(8,128)S(1)} fusion(f32[128,8,4096]{2,0,1:T(8,128)S(1)} %get-tuple-element.25, f32[128,8]{0,1:T(8,128)S(1)} %get-tuple-element.24, pred[4096]{0:T(1024)(128)(4,1)S(1)} %compare_or_fusion), kind=kLoop, calls=%fused_computation.2 | loop fusion | flops 20970496 | bytes 16789504 | tf_op jit(solution)/shard_map/reduce_sum | solution.py:56
  84.7 35.6 %all-gather.5.cloned.1.call-done = bf16[4096,1,128]{0,2,1:T(8,128)(2,1)} async-done(((bf16[128,1,128]{0,2,1:T(8,128)(2,1)}), bf16[4096,1,128]{0,2,1:T(8,128)(2,1)}) %all-gather.5.cloned.1.call-update) | async-done | bytes 1048592 | tf_op jit(solution)/shard_map/all_gather | solution.py:41
  120.4 9.2 %fusion.15 = (f32[128,8]{0,1:T(8,128)S(1)}, bf16[128,8,128]{0,2,1:T(8,128)(2,1)S(1)}) fusion(bf16[128,8,128]{0,2,1:T(8,128)(2,1)S(1)} %copy.56, pred[128]{0:T(512)(128)(4,1)S(1)} %get-tuple-element.21, f32[128]{0:T(128)S(1)} %get-tuple-element.20, bf16[4096,1,128]{0,2,1:T(8,128)(2,1)} %all-gather.5.cloned.1.call-done, f32[128,8,4096]{2,0,1:T(8,128)} %copy-done, ...), kind=kOutput, calls=%fused_computation.24 | convolution fusion | flops 1095498752 | bytes 18363008 | tf_op jit(solution)/shard_map/gtrs,sgd->tgrd/dot_general | solution.py:60
  129.6 1.6 copy-done.1
  131.4 7.7 %multiply_convert_fusion = bf16[128,8,4096]{2,0,1:T(8,128)(2,1)} fusion(f32[128,8,4096]{2,0,1:T(8,128)S(1)} %copy-done.1, f32[128,8]{0,1:T(8,128)S(1)} %get-tuple-element.22, f32[128,8]{0,1:T(8,128)S(1)} %log_add_fusion, pred[4096]{0:T(1024)(128)(4,1)S(1)} %compare_or_fusion, bf16[4096,1,128]{0,2,1:T(8,128)(2,1)S(1)} %copy-done.4, ...), kind=kOutput, calls=%fused_computation | convolution fusion | flops 1103233024 | bytes 26488960 | tf_op jit(solution)/shard_map/tgrd,sgd->gtrs/dot_general | solution.py:65
  139.2 6.8 %fusion.6 = bf16[4096,1,128]{2,0,1:T(8,128)(2,1)} fusion(bf16[128,8,4096]{2,0,1:T(8,128)(2,1)} %multiply_convert_fusion, bf16[128,8,128]{2,1,0:T(8,128)(2,1)S(1)} %copy-done.3), kind=kOutput, calls=%fused_computation.12 | convolution fusion | flops 1074790400 | bytes 9699328 | tf_op jit(solution)/shard_map/gtrs,tgrd->sgd/dot_general | solution.py:75
  146.2 8.0 %fusion.5 = bf16[4096,128]{0,1:T(8,128)(2,1)S(1)} fusion(bf16[128,8,128]{0,2,1:T(8,128)(2,1)S(1)} %copy.56, pred[128]{0:T(512)(128)(4,1)S(1)} %get-tuple-element.21, f32[128,8,4096]{2,0,1:T(8,128)} %copy-done, f32[128,8]{0,1:T(8,128)S(1)} %log_add_fusion, pred[4096]{0:T(1024)(128)(4,1)S(1)} %compare_or_fusion), kind=kOutput, calls=%fused_computation.11 | convolution fusion | flops 1095368704 | bytes 18096256 | tf_op jit(solution)/shard_map/gtrs,tgrd->sgd/dot_general | solution.py:78
  154.2 1.3 copy.74
  155.6 73.1 %reduce-scatter.5.cloned.1.call-done = bf16[128,1,128]{2,0,1:T(8,128)(2,1)} async-done(((bf16[4096,1,128]{2,0,1:T(8,128)(2,1)}), bf16[128,1,128]{2,0,1:T(8,128)(2,1)}) %reduce-scatter.5.cloned.1.call-update) | async-done | bytes 32784 | tf_op jit(solution)/shard_map/reduce_scatter | solution.py:82
  229.2 1.4 reduce.5
  231.2 6.7 %all-to-all-start.2 = ((bf16[8,2,1024]{2,1,0:T(2,128)(2,1)}), bf16[8,2,1024]{2,1,0:T(2,128)(2,1)S(1)}, u32[]{:S(2)}, u32[]{:S(2)}) async-start(bf16[8,2,1024]{2,1,0:T(2,128)(2,1)} %reshape.206), calls=%async_computation.3 | async-start | bytes 65536 | tf_op jit(solution)/shard_map/all_to_all | solution.py:90
  238.0 79.4 %reduce-scatter.7.cloned.1.call-done = bf16[128,128]{1,0:T(8,128)(2,1)} async-done(((bf16[4096,128]{1,0:T(8,128)(2,1)}), bf16[128,128]{1,0:T(8,128)(2,1)}) %reduce-scatter.7.cloned.1.call-update) | async-done | bytes 32784
  317.3 0.9 copy.75
  318.2 0.7 reduce.6
  319.6 6.8 %all-to-all-start.3 = ((bf16[8,2,1024]{2,1,0:T(2,128)(2,1)}), bf16[8,2,1024]{2,1,0:T(2,128)(2,1)S(1)}, u32[]{:S(2)}, u32[]{:S(2)}) async-start(bf16[8,2,1024]{2,1,0:T(2,128)(2,1)} %reshape.208), calls=%async_computation.4 | async-start | bytes 65536 | tf_op jit(solution)/shard_map/all_to_all | solution.py:93
  326.4 5.7 %fusion.9 = bf16[128,8,128]{2,0,1:T(8,128)(2,1)S(1)} fusion(bf16[128,8,4096]{2,0,1:T(8,128)(2,1)} %multiply_convert_fusion, bf16[4096,1,128]{2,0,1:T(8,128)(2,1)S(1)} %copy-done.2), kind=kOutput, calls=%fused_computation.17 | convolution fusion | flops 1074003968 | bytes 9699328 | tf_op jit(solution)/shard_map/gtrs,sgd->tgrd/dot_general | solution.py:70
  332.1 0.9 copy.65
  333.0 0.9 copy.66
  334.0 0.7 copy.83
  (32 shorter events, 3.5 us)
Async XLA Ops:
  7.2 62.8 %all-gather.3.cloned.1.call-start = ((), (), s32[]{:S(2)}) async-start(), calls=%async_computation.6 | async-start | bytes 1081344 | tf_op jit(solution)/shard_map/all_gather | solution.py:40
  25.2 10.1 %all-to-all-start.1 = ((bf16[16,8,128]{2,0,1:T(8,128)(2,1)}), bf16[16,8,128]{2,0,1:T(8,128)(2,1)S(1)}, u32[]{:S(2)}, u32[]{:S(2)}) async-start(bf16[16,8,128]{2,0,1:T(8,128)(2,1)} %copy.54), calls=%async_computation.1 | async-start | bytes 65536 | tf_op jit(solution)/shard_map/all_to_all | solution.py:37
  28.5 91.9 %all-gather.5.cloned.1.call-start = ((), (), s32[]{:S(2)}) async-start(), calls=%async_computation.7 | async-start | bytes 1081344 | tf_op jit(solution)/shard_map/all_gather | solution.py:41
  36.1 192.6 %reduce-scatter.5.cloned.1.call-start = ((), (), s32[]{:S(2)}) async-start(), calls=%async_computation.8 | async-start | bytes 1081344 | tf_op jit(solution)/shard_map/reduce_scatter | solution.py:82
  74.1 5.7 %copy-start = (f32[128,8,4096]{2,0,1:T(8,128)}, f32[128,8,4096]{2,0,1:T(8,128)S(1)}, u32[]{:S(2)}) copy-start(f32[128,8,4096]{2,0,1:T(8,128)S(1)} %get-tuple-element.25) | copy-start | bytes 50331652
  120.4 10.8 %copy-start.1 = (f32[128,8,4096]{2,0,1:T(8,128)S(1)}, f32[128,8,4096]{2,0,1:T(8,128)}, u32[]{:S(2)}) copy-start(f32[128,8,4096]{2,0,1:T(8,128)} %copy-done) | copy-start | bytes 50331652
  120.4 11.1 %copy-start.4 = (bf16[4096,1,128]{0,2,1:T(8,128)(2,1)S(1)}, bf16[4096,1,128]{0,2,1:T(8,128)(2,1)}, u32[]{:S(2)}) copy-start(bf16[4096,1,128]{0,2,1:T(8,128)(2,1)} %all-gather.5.cloned.1.call-done) | copy-start | bytes 3145732
  131.4 7.7 %copy-start.3 = (bf16[128,8,128]{2,1,0:T(8,128)(2,1)S(1)}, bf16[128,8,128]{2,1,0:T(8,128)(2,1)}, u32[]{:S(2)}) copy-start(bf16[128,8,128]{2,1,0:T(8,128)(2,1)} %param.6) | copy-start | bytes 786436
  146.0 180.4 %copy-start.2 = (bf16[4096,1,128]{2,0,1:T(8,128)(2,1)S(1)}, bf16[4096,1,128]{2,0,1:T(8,128)(2,1)}, u32[]{:S(2)}) copy-start(bf16[4096,1,128]{2,0,1:T(8,128)(2,1)} %all-gather.3.cloned.1.call-done) | copy-start | bytes 3145732
  146.0 171.4 %reduce-scatter.7.cloned.1.call-start = ((), (), s32[]{:S(2)}) async-start(), calls=%async_computation.9 | async-start | bytes 1081344
  231.2 88.4 %all-to-all-start.2 = ((bf16[8,2,1024]{2,1,0:T(2,128)(2,1)}), bf16[8,2,1024]{2,1,0:T(2,128)(2,1)S(1)}, u32[]{:S(2)}, u32[]{:S(2)}) async-start(bf16[8,2,1024]{2,1,0:T(2,128)(2,1)} %reshape.206), calls=%async_computation.3 | async-start | bytes 65536 | tf_op jit(solution)/shard_map/all_to_all | solution.py:90
  319.6 15.0 %all-to-all-start.3 = ((bf16[8,2,1024]{2,1,0:T(2,128)(2,1)}), bf16[8,2,1024]{2,1,0:T(2,128)(2,1)S(1)}, u32[]{:S(2)}, u32[]{:S(2)}) async-start(bf16[8,2,1024]{2,1,0:T(2,128)(2,1)} %reshape.208), calls=%async_computation.4 | async-start | bytes 65536 | tf_op jit(solution)/shard_map/all_to_all | solution.py:93
Sparse Core Ops, SparseCore 0:
  23.9 45.9 all-gather.2
  73.0 47.3 all-gather.4
  146.1 82.5 reduce-scatter.4
  232.8 84.4 reduce-scatter.6
where the time goes:
time: 344 us; the launch traced here: 342 us
  waiting for transfers between devices  225 us (65%)
  matrix products  41.6 us (12%)
  local copies, waits for them, and re-layouts  20 us (6%)
  starting transfers between devices  17.2 us (5%)
  blocking collectives  15.8 us (5%)
  between operations  13.9 us (4%)
  other arithmetic  8.56 us (2%)
    unnamed x5, waiting for transfers between devices  79.4 us
    reduce_scatter x1, waiting for transfers between devices, on_device(): lax.psum_scatter(key_part.astype(jnp.bfloat16), 'prefix', scatter_dimensi...  73.1 us
    all_gather x1, waiting for transfers between devices, on_device(): lax.all_gather(owned_values, 'prefix', axis=0, tiled=True)  35.6 us
    all_gather x1, waiting for transfers between devices, on_device(): lax.all_gather(owned_keys, 'prefix', axis=0, tiled=True)  33.8 us
    unnamed x23, local copies, waits for them, and re-layouts  16.9 us
    all_to_all x1, blocking collectives, on_device(): lax.all_to_all(prefix_keys, 'group', split_axis=1, concat_axis=0, tiled=T...  15.8 us
    dot_general x1, matrix products, on_device(): jnp.einsum('gtrs,sgd->tgrd', weights, all_values, preferred_element_type=...  9.22 us
    dot_general x1, matrix products, on_device(): jnp.einsum('gtrs,tgrd->sgd', weights, grad_four, preferred_element_type=j...  8.04 us
  transfers between devices with their start and end apart: 7, of which 5 were waited for; matrix products, arithmetic and copies ran while one was open for 11% of the time, Pallas kernels for 0%

commit v1 on v0

v1 whole, which is shorter than its diff:
```python
import functools
import math

import jax
import jax.numpy as jnp
from jax import lax
from jax.experimental import pallas as pl
from jax.experimental.pallas import tpu as pltpu
from jax.sharding import PartitionSpec as P

F32, BF16 = jnp.float32, jnp.bfloat16
MESH = pl.DeviceIdType.MESH
NZ, NX = 8, 4


class Place:
    def __init__(self):
        self.z = lax.axis_index("group")
        p = lax.axis_index("prefix")
        self.x, self.y, self.c = p // 8, p // 2 % 4, p % 2
        c = self.c
        self.a = self.x + c * (self.y - self.x)
        self.b = self.y + c * (self.x - self.y)

    def xy(self, a, b):
        c = self.c
        return a + c * (b - a), b + c * (a - b)

    def at(self, a, b):
        x, y = self.xy(a, b)
        return (self.z, (x * 4 + y) * 2 + self.c)

    def chip(self, z, c):
        return (z, (self.x * 4 + self.y) * 2 + c)


def greet(me):
    barrier = pltpu.get_barrier_semaphore()
    a, b, z, c = me.a, me.b, me.z, me.c
    devs = [me.at((a + o) % 4, b) for o in (1, 2, 3)] + [me.at(a, (b + o) % 4) for o in (1, 2, 3)]
    devs += [me.chip((z + d) % NZ, (c + r) % 2) for d in range(NZ) for r in range(2) if d or r]
    for d in devs:
        pl.semaphore_signal(barrier, inc=1, device_id=d, device_id_type=MESH)
    pl.semaphore_wait(barrier, len(devs))


def rcopy(src, dst, ss, rs, dev):
    return pltpu.make_async_remote_copy(src_ref=src, dst_ref=dst, send_sem=ss, recv_sem=rs,
                                        device_id=dev, device_id_type=MESH)


def gather_kernel(k_ref, v_ref, kv, f32buf, sendbuf, z_send, z_recv,
                  a_send, a_recv, b_send, b_recv, s_send, s_recv):
    me = Place()
    a, b, z, c = me.a, me.b, me.z, me.c
    for i, ref in enumerate((k_ref, v_ref)):
        f32buf[i] = ref[...].astype(F32).reshape(128, 128)
    for i in range(2):
        for h in range(NZ):
            sendbuf[i, h] = f32buf[i, pl.ds(h, 16, stride=8), :].astype(BF16)
    greet(me)
    strip = pl.ds(pl.multiple_of(c * 16, 16), 16)
    for d in range(NZ):
        h = (z + d) % NZ
        for r in range(2):
            ct = (c + r) % 2
            src, dst = sendbuf.at[ct, h], kv.at[ct, z, me.x, me.y, strip]
            if d or r:
                rcopy(src, dst, z_send.at[r], z_recv, me.chip(h, ct)).start()
            else:
                pltpu.make_async_copy(src, dst, z_recv).start()

    def blk(i, j, lo=0, n=8):
        x, y = me.xy(i, j)
        return kv.at[c, pl.ds(lo, n), x, y]

    sib = me.chip(z, 1 - c)
    sends = []

    def send(ref, ss, rs, dev):
        cp = rcopy(ref, ref, ss, rs, dev)
        cp.start()
        sends.append(cp)

    def wait(ref, rs):
        pltpu.make_async_copy(ref, ref, rs).wait()

    def sibling(ref):
        rcopy(ref, ref, s_send, s_recv, sib).start()

    near = (3, 1, 2)

    def along_b(k):
        ref = blk((a + cols[k]) % 4, b)
        for i, o in enumerate(near):
            send(ref, b_send.at[i, k], b_recv.at[i, k], me.at(a, (b + 4 - o) % 4))
        sibling(ref)

    def arrived(k):
        for i, o in enumerate(near):
            ref = blk((a + cols[k]) % 4, (b + o) % 4)
            wait(ref, b_recv.at[i, k])
            sibling(ref)

    cols = (0, 3, 1, 2)
    own = blk(a, b)
    wait(own, z_recv)
    for i, o in enumerate(near):
        send(own, a_send.at[i], a_recv.at[i], me.at((a + 4 - o) % 4, b))
    along_b(0)
    for k in range(1, 4):
        wait(blk((a + cols[k]) % 4, b), a_recv.at[k - 1])
        along_b(k)
    for k in range(4):
        arrived(k)
    other = kv.at[1 - c]
    wait(other, s_recv)
    wait(sendbuf.at[0, pl.ds(0, 7)], z_send.at[0])
    wait(sendbuf.at[0], z_send.at[1])
    wait(other, s_send)
    for cp in sends:
        cp.wait_send()


def gather(keys, values, space=pl.ANY):
    vm = pl.BlockSpec(memory_space=pltpu.VMEM)
    dma = pltpu.SemaphoreType.DMA
    return pl.pallas_call(
        gather_kernel,
        out_shape=jax.ShapeDtypeStruct((2, NZ, NX, NX, 32, 128), BF16),
        in_specs=[vm, vm],
        out_specs=pl.BlockSpec(memory_space=space),
        scratch_shapes=[
            pltpu.VMEM((2, 128, 128), F32), pltpu.VMEM((2, NZ, 16, 128), BF16),
            dma((2,)), dma, dma((3,)), dma((3,)), dma((3, 4)), dma((3, 4)), dma, dma,
        ],
        compiler_params=pltpu.CompilerParams(collective_id=0, has_side_effects=True),
        name="gather_heads",
    )(keys, values)


def scatter_kernel(g_ref, out, sbuf, bbuf, abuf, w, zbuf, s_send, s_recv, b_send, b_recv,
                   a_send, a_recv, z_send, z_recv):
    me = Place()
    a, b, z, c = me.a, me.b, me.z, me.c
    sib = me.chip(z, 1 - c)
    greet(me)
    sends = []

    def blk(kind, da, db):
        x, y = me.xy((a + da) % 4, (b + db) % 4)
        return kind, slice(None), x, y

    def send(src, dst, ss, rs, dev):
        cp = rcopy(src, dst, ss, rs, dev)
        cp.start()
        sends.append(cp)

    def wait(ref, rs):
        pltpu.make_async_copy(ref, ref, rs).wait()

    steps = [(da, db) for db in (2, 1, 3, 0) for da in (2, 1, 3, 0)]
    for da, db in steps:
        oa = me.x + (1 - c) * (me.y - me.x)
        ob = me.y + (1 - c) * (me.x - me.y)
        ta, tb = (oa + da) % 4, (ob + db) % 4
        tx = ta + (1 - c) * (tb - ta)
        ty = tb + (1 - c) * (ta - tb)
        send(g_ref.at[1 - c, :, tx, ty], sbuf.at[da, db], s_send.at[da, db], s_recv.at[da, db], sib)

    def f32(v):
        return v.astype(F32)

    for da, db in steps:
        wait(sbuf.at[da, db], s_recv.at[da, db])
        if db:
            sbuf[da, db] = (f32(sbuf[da, db]) + f32(g_ref[blk(c, da, db)])).astype(BF16)
            send(sbuf.at[da, db], bbuf.at[db - 1, da], b_send.at[db - 1, da], b_recv.at[db - 1, da],
                 me.at(a, (b + db) % 4))
            continue
        for i in range(3):
            wait(bbuf.at[i, da], b_recv.at[i, da])
        total = f32(sbuf[da, db]) + f32(g_ref[blk(c, da, db)]) + f32(bbuf[0, da]) + f32(bbuf[1, da]) + f32(bbuf[2, da])
        if da:
            sbuf[da, db] = total.astype(BF16)
            send(sbuf.at[da, db], abuf.at[da - 1], a_send.at[da - 1], a_recv.at[da - 1], me.at((a + da) % 4, b))
            continue
        for i in range(3):
            wait(abuf.at[i], a_recv.at[i])
        total = total + f32(abuf[0]) + f32(abuf[1]) + f32(abuf[2])
        w[...] = total.astype(BF16)
    for d in range(NZ):
        t = (z + d) % NZ
        for r in range(2):
            ct = (c + r) % 2
            src, dst = w.at[t, pl.ds(pl.multiple_of(ct * 16, 16), 16)], zbuf.at[c, z]
            if d or r:
                rcopy(src, dst, z_send.at[r], z_recv, me.chip(t, ct)).start()
            else:
                pltpu.make_async_copy(src, dst, z_recv).start()
    wait(zbuf, z_recv)
    for i in range(2):
        for h in range(NZ):
            out[i, pl.ds(h, 16, stride=8), :] = f32(zbuf[i, h])
    wait(zbuf.at[0, pl.ds(0, 7)], z_send.at[0])
    wait(zbuf.at[0], z_send.at[1])
    for cp in sends:
        cp.wait_send()


def scatter(g):
    vm = pl.BlockSpec(memory_space=pltpu.VMEM)
    dma = pltpu.SemaphoreType.DMA
    return pl.pallas_call(
        scatter_kernel,
        out_shape=jax.ShapeDtypeStruct((2, 128, 128), F32),
        in_specs=[vm],
        out_specs=vm,
        scratch_shapes=[
            pltpu.VMEM((4, 4, NZ, 32, 128), BF16), pltpu.VMEM((3, 4, NZ, 32, 128), BF16),
            pltpu.VMEM((3, NZ, 32, 128), BF16), pltpu.VMEM((NZ, 32, 128), BF16), pltpu.VMEM((2, NZ, 16, 128), BF16),
            dma((4, 4)), dma((4, 4)), dma((3, 4)), dma((3, 4)), dma((3,)), dma((3,)), dma((2,)), dma,
        ],
        compiler_params=pltpu.CompilerParams(collective_id=1, has_side_effects=True, vmem_limit_bytes=32 * 2**20),
        name="scatter_heads",
    )(g)


TILE = 128
C2 = (1.0 / math.sqrt(128)) * math.log2(math.e)
IR = 1.0 / math.sqrt(128)
NT = (((1,), (1,)), ((), ()))


def dot(a, b):
    return jnp.dot(a, b, preferred_element_type=F32)


def dot_nt(a, b):
    return lax.dot_general(a, b, NT, preferred_element_type=F32)


def compute_kernel(mask_ref, nval_ref, q_ref, g_ref, kv_ref,
                   att_ref, qg_ref, kvg_ref,
                   kc, vo, s_buf, p_buf, m_buf, acc, qg_acc, g0, qT, gT, idx, *, chunk):
    R = q_ref.shape[0]
    T = mask_ref.shape[0]
    tpc = chunk // TILE
    nchunks = T // tpc
    def scan(t, n):
        seen = jnp.logical_or(mask_ref[t] == 1, t == 0)

        @pl.when(seen)
        def _():
            idx[n] = t
            kc[pl.ds(pl.multiple_of(n * TILE, TILE), TILE), :] = kv_ref[0, pl.ds(pl.multiple_of(t * TILE, TILE), TILE), :]
            vo[pl.ds(pl.multiple_of(n * TILE, TILE), TILE), 0:128] = kv_ref[1, pl.ds(pl.multiple_of(t * TILE, TILE), TILE), :]
            vo[pl.ds(pl.multiple_of(n * TILE, TILE), TILE), 128:256] = jnp.ones((TILE, 128), BF16)

        @pl.when(jnp.logical_not(seen))
        def _():
            kvg_ref[0, pl.ds(pl.multiple_of(t * TILE, TILE), TILE), :] = jnp.zeros((TILE, 128), BF16)
            kvg_ref[1, pl.ds(pl.multiple_of(t * TILE, TILE), TILE), :] = jnp.zeros((TILE, 128), BF16)
        return n + seen.astype(jnp.int32)

    n = lax.fori_loop(0, T, scan, jnp.int32(0))
    nc = (n + tpc - 1) // tpc

    def pad(t, _):
        kc[pl.ds(pl.multiple_of(t * TILE, TILE), TILE), :] = kv_ref[0, 0:TILE, :]
        vo[pl.ds(pl.multiple_of(t * TILE, TILE), TILE), :] = jnp.zeros((TILE, 256), BF16)
        return 0
    lax.fori_loop(n, nc * tpc, pad, 0)

    nrow = nval_ref[0] * 8
    rows = lax.broadcasted_iota(jnp.int32, (R, 128), 0)
    valid = rows < nrow
    g0[...] = jnp.where(valid, g_ref[...].astype(F32), 0.0).astype(BF16)

    m_buf[...] = jnp.full((R, 128), -jnp.inf, F32)

    def crow(c):
        return pl.ds(pl.multiple_of(c * chunk, chunk), chunk)

    RB = 256

    def ph1(c, _):
        kk = kc[crow(c), :]
        for r in range(0, R, RB):
            s = dot_nt(q_ref[r:r + RB, :], kk)
            s_buf[c, r:r + RB, :] = s
            mm = s[:, 0:128]
            for j in range(1, tpc):
                mm = jnp.maximum(mm, s[:, j * 128:(j + 1) * 128])
            m_buf[r:r + RB, :] = jnp.maximum(m_buf[r:r + RB, :], mm)
        return 0
    lax.fori_loop(0, nc, ph1, 0)
    m_buf[...] = jnp.broadcast_to(jnp.max(m_buf[...], axis=1, keepdims=True), (R, 128))

    acc[...] = jnp.zeros((R, 256), F32)

    def ph2(c, _):
        vv = vo[crow(c), :]
        for r in range(0, R, RB):
            m = m_buf[r:r + RB, 0:1]
            p = jnp.exp2((s_buf[c, r:r + RB, :] - m) * C2).astype(BF16)
            p_buf[c, r:r + RB, :] = p
            acc[r:r + RB, :] += dot(p, vv)
        return 0
    lax.fori_loop(0, nc, ph2, 0)

    l = acc[:, 128:256]
    rl = 1.0 / l
    mixed = jnp.where(valid, acc[:, 0:128] * rl, 0.0)
    att_ref[...] = mixed.astype(BF16)
    gf = g0[...].astype(F32)
    off = jnp.sum(gf * mixed, axis=1, keepdims=True)
    m_buf[...] = jnp.broadcast_to(off, (R, 128))
    qT[...] = jnp.transpose(q_ref[...].astype(F32) * (rl * IR)).astype(BF16)
    gT[...] = jnp.transpose(gf * rl).astype(BF16)
    qg_acc[...] = jnp.zeros((R, 128), F32)

    def unpad(t, _):
        kc[pl.ds(pl.multiple_of(t * TILE, TILE), TILE), :] = jnp.zeros((TILE, 128), BF16)
        return 0
    lax.fori_loop(n, nc * tpc, unpad, 0)

    def ph3(c, _):
        vv = vo[crow(c), 0:128]
        kk = kc[crow(c), :]
        kgT = jnp.zeros((128, chunk), F32)
        vgT = jnp.zeros((128, chunk), F32)
        for r in range(0, R, RB):
            vd = dot_nt(g0[r:r + RB, :], vv)
            p = p_buf[c, r:r + RB, :]
            ds = (p.astype(F32) * (vd - m_buf[r:r + RB, 0:1])).astype(BF16)
            qg_acc[r:r + RB, :] += dot(ds, kk)
            kgT += dot(qT[:, r:r + RB], ds)
            vgT += dot(gT[:, r:r + RB], p)
        kg = jnp.transpose(kgT).astype(BF16)
        vg = jnp.transpose(vgT).astype(BF16)
        for j in range(tpc):
            pos = c * tpc + j

            @pl.when(pos < n)
            def _():
                t = idx[pos]
                kvg_ref[0, pl.ds(pl.multiple_of(t * TILE, TILE), TILE), :] = kg[j * TILE:(j + 1) * TILE, :]
                kvg_ref[1, pl.ds(pl.multiple_of(t * TILE, TILE), TILE), :] = vg[j * TILE:(j + 1) * TILE, :]
        return 0
    lax.fori_loop(0, nc, ph3, 0)
    rl = 1.0 / acc[:, 128:256]
    qg_ref[...] = (qg_acc[...] * (rl * IR)).astype(BF16)


def compute(mask_row, nval, q, g, kv, chunk=512):
    R = q.shape[0]
    S = kv.shape[1]
    sm = pl.BlockSpec(memory_space=pltpu.SMEM)
    vm = pl.BlockSpec(memory_space=pltpu.VMEM)
    return pl.pallas_call(
        functools.partial(compute_kernel, chunk=chunk),
        out_shape=(jax.ShapeDtypeStruct((R, 128), BF16), jax.ShapeDtypeStruct((R, 128), BF16),
                   jax.ShapeDtypeStruct((2, S, 128), BF16)),
        in_specs=[sm, sm, vm, vm, vm],
        out_specs=(vm, vm, vm),
        scratch_shapes=[
            pltpu.VMEM((S, 128), BF16), pltpu.VMEM((S, 256), BF16),
            pltpu.VMEM((S // chunk, R, chunk), F32), pltpu.VMEM((S // chunk, R, chunk), BF16),
            pltpu.VMEM((R, 128), F32), pltpu.VMEM((R, 256), F32), pltpu.VMEM((R, 128), F32),
            pltpu.VMEM((R, 128), BF16), pltpu.VMEM((128, R), BF16), pltpu.VMEM((128, R), BF16),
            pltpu.SMEM((S // TILE,), jnp.int32),
        ],
        compiler_params=pltpu.CompilerParams(vmem_limit_bytes=60 * 2**20),
        name="attend",
    )(mask_row, nval, q, g, kv)


def on_device(queries, prefix_keys, prefix_values, out_grad, tile_mask, lengths):
    tok = queries.shape[0]
    span = 2048
    first = lax.axis_index("prefix") * tok
    comp = first // span
    nval = jnp.clip(lax.dynamic_index_in_dim(lengths, comp, 0, keepdims=True) - first % span, 0, tok)
    mask_row = lax.dynamic_index_in_dim(tile_mask, comp, 0, keepdims=False)
    kv = gather(prefix_keys, prefix_values).reshape(2, -1, 128)
    q, g = queries.reshape(-1, 128), out_grad.reshape(-1, 128)
    att, qg, kvg = compute(mask_row, nval, q, g, kv)
    out = scatter(kvg.reshape(2, NZ, NX, NX, 32, 128)).reshape(2, 16, 8, 128)
    return att.reshape(queries.shape), qg.reshape(queries.shape), out[0], out[1]


def solution(mesh):
    tokens, owned = P("prefix", "group", None), P(("group", "prefix"), None, None)
    return jax.shard_map(
        on_device,
        mesh=mesh,
        in_specs=(tokens, owned, owned, tokens, P(), P()),
        out_specs=(tokens, tokens, owned, owned),
        check_vma=False,
    )
```

time: 344 us -> 74.1 us (0.22)
  waiting for transfers between devices: 225 us -> 0 us
  Pallas kernels: 0 us -> 68.5 us
  matrix products: 41.6 us -> 0 us
  starting transfers between devices: 17.2 us -> 0 us
  local copies, waits for them, and re-layouts: 20 us -> 4.02 us
  blocking collectives: 15.8 us -> 0 us
  between operations: 13.9 us -> 1.35 us
  other arithmetic: 8.56 us -> 0 us
    unnamed x5 -> x0, waiting for transfers between devices: 79.4 us -> none
    reduce_scatter x1 -> x0, waiting for transfers between devices: 73.1 us -> none  [on_device(): lax.psum_scatter(key_part.astype(jnp.bfloat16), 'prefix', scatter_dimensi...]
    all_gather x2 -> x0, waiting for transfers between devices: 69.5 us -> none  [the longest x1 35.6 us: on_device(): lax.all_gather(owned_values, 'prefix', axis=0, tiled=True)]
    pallas_call x0 -> x3, Pallas kernels: none -> 68.5 us  [the longest x1 30.1 us: gather(): pl.pallas_call(gather_kernel, out_shape=jax.ShapeDtypeStruct((2, NZ, NX,...]
    dot_general x6 -> x0, matrix products: 41.6 us -> none  [the longest x1 9.22 us: on_device(): jnp.einsum('gtrs,sgd->tgrd', weights, all_values, preferred_element_type=...]
    all_to_all x3 -> x0, starting transfers between devices: 16.8 us -> none  [the longest x1 6.76 us: on_device(): lax.all_to_all(value_sum.astype(jnp.bfloat16), 'group', split_axis=0, con...]
    all_to_all x1 -> x0, blocking collectives: 15.8 us -> none  [on_device(): lax.all_to_all(prefix_keys, 'group', split_axis=1, concat_axis=0, tiled=T...]
    unnamed x23 -> x4, local copies, waits for them, and re-layouts: 16.9 us -> 1.6 us
  transfers between devices with their start and end apart: 7 -> 0, of which waited for: 5 -> 0; matrix products, arithmetic and copies ran while one was open for 11% -> 0% of each run, Pallas kernels for 0% -> 0%
where the time goes in v1:
time: 74.1 us; the launch traced here: 73.8 us
  Pallas kernels  68.5 us (92%)
  local copies, waits for them, and re-layouts  4.02 us (5%)
  between operations  1.35 us (2%)
    pallas_call x1, Pallas kernels, gather(): pl.pallas_call(gather_kernel, out_shape=jax.ShapeDtypeStruct((2, NZ, NX,...  30.1 us
    pallas_call x1, Pallas kernels, scatter(): pl.pallas_call(scatter_kernel, out_shape=jax.ShapeDtypeStruct((2, 128, 12...  21.2 us
    pallas_call x1, Pallas kernels, compute(): pl.pallas_call(functools.partial(compute_kernel, chunk=chunk), out_shape=...  17.2 us
    unnamed x4, local copies, waits for them, and re-layouts  1.6 us

profile of v1, /device:TPU:1, one launch (start us, length us, event | category | flops | bytes accessed | tf_op | source)
XLA Modules:
  0.0 73.8 jit_solution(15293479197033975691)
XLA Ops:
  0.6 0.0 copy-start
  0.7 1.2 %dynamic_slice.9 = s32[1]{0:T(128)} dynamic-slice(s32[2]{0:T(128)} %param.11, s32[]{:T(128)S(6)} %select_n.18), dynamic_slice_sizes={1} | dynamic-slice | bytes 12 | tf_op jit(solution)/shard_map/jit(dynamic_index_in_dim)/dynamic_slice | solution.py:384
  2.6 0.0 copy-done
  2.6 0.5 dynamic-slice_bitcast_fusion.mask_ref
  3.1 30.1 %gather_heads.1 = bf16[2,8,4,4,32,128]{5,4,3,2,1,0:T(8,128)(2,1)} custom-call(bf16[16,8,128]{2,1,0:T(8,128)(2,1)} %k_ref.1, bf16[16,8,128]{2,1,0:T(8,128)(2,1)} %v_ref.1), custom_call_target="tpu_custom_call" | custom-call | tf_op jit(solution)/shard_map/gather_heads/pallas_call | solution.py:128
  33.2 17.2 %attend.1 = (bf16[1024,128]{1,0:T(8,128)(2,1)}, bf16[1024,128]{1,0:T(8,128)(2,1)}, bf16[2,4096,128]{2,1,0:T(8,128)(2,1)}) custom-call(s32[32]{0:T(128)} %dynamic-slice_bitcast_fusion.mask_ref, s32[1]{0:T(128)S(6)} %min.6.nval_ref, bf16[1024,128]{1,0:T(8,128)(2,1)} %bitcast.15, bf16[1024,128]{1,0:T(8,128)(2,1)} %bitcast.16, bf16[2,4096,128]{2,1,0:T(8,128)(2,1)} %bitcast.14), custom_call_target="tpu_custom_call" | custom-call | tf_op jit(solution)/shard_map/attend/pallas_call | solution.py:361
  50.4 0.0 copy-start.1
  50.4 1.6 %copy-done.1 = bf16[2,4096,128]{2,1,0:T(8,128)(2,1)S(1)} copy-done((bf16[2,4096,128]{2,1,0:T(8,128)(2,1)S(1)}, bf16[2,4096,128]{2,1,0:T(8,128)(2,1)}, u32[]{:S(2)}) %copy-start.1) | copy-done | bytes 2097176
  52.0 21.2 %scatter_heads.1 = f32[2,128,128]{2,1,0:T(8,128)S(1)} custom-call(bf16[2,8,4,4,32,128]{5,4,3,2,1,0:T(8,128)(2,1)S(1)} %bitcast.13), custom_call_target="tpu_custom_call" | custom-call | tf_op jit(solution)/shard_map/scatter_heads/pallas_call | solution.py:214
  73.2 0.7 slice_bitcast_fusion
Async XLA Ops:
  0.6 1.9 %copy-start = (s32[2,32]{1,0:T(2,128)S(1)}, s32[2,32]{1,0:T(2,128)}, u32[]{:S(2)}) copy-start(s32[2,32]{1,0:T(2,128)} %param.10) | copy-start | bytes 772
  50.4 1.6 %copy-start.1 = (bf16[2,4096,128]{2,1,0:T(8,128)(2,1)S(1)}, bf16[2,4096,128]{2,1,0:T(8,128)(2,1)}, u32[]{:S(2)}) copy-start(bf16[2,4096,128]{2,1,0:T(8,128)(2,1)} %get-tuple-element.9) | copy-start | bytes 6291460

commit v2 on v0

v2 whole, which is shorter than its diff:
```python
import functools
import math

import jax
import jax.numpy as jnp
from jax import lax
from jax.experimental import pallas as pl
from jax.experimental.pallas import tpu as pltpu
from jax.sharding import PartitionSpec as P

F32, BF16 = jnp.float32, jnp.bfloat16
MESH = pl.DeviceIdType.MESH
NZ = 8
BLK = 256
SPAN = 2048
ROOT = 1.0 / math.sqrt(128)
C2 = ROOT * math.log2(math.e)
HIDDEN = -1e30

STEPS = [(2, 2), (1, 1), (3, 3), (2, 1), (1, 2), (2, 3), (3, 2), (1, 3), (3, 1),
         (2, 0), (0, 2), (1, 0), (0, 1), (3, 0), (0, 3), (0, 0)]
FAR, NEAR = range(0, 9), range(9, 16)
RING = (3, 1, 2)
COLS = (0, 3, 1, 2)


class Place:
    def __init__(self):
        self.z = lax.axis_index("group")
        p = lax.axis_index("prefix")
        self.x, self.y, self.c = p // 8, p // 2 % 4, p % 2
        self.a, self.b = self.turn(self.x, self.y)

    def turn(self, u, v):
        return u + self.c * (v - u), v + self.c * (u - v)

    def turn_other(self, u, v):
        return u + (1 - self.c) * (v - u), v + (1 - self.c) * (u - v)

    def at(self, a, b):
        x, y = self.turn(a, b)
        return (self.z, (x * 4 + y) * 2 + self.c)

    def chip(self, z, c):
        return (z, (self.x * 4 + self.y) * 2 + c)


def rcopy(src, dst, ss, rs, dev):
    return pltpu.make_async_remote_copy(src_ref=src, dst_ref=dst, send_sem=ss, recv_sem=rs,
                                        device_id=dev, device_id_type=MESH)


def wait(ref, sem):
    pltpu.make_async_copy(ref, ref, sem).wait()


def dot(u, v):
    return jnp.dot(u, v, preferred_element_type=F32)


def dot_nt(u, v):
    return lax.dot_general(u, v, (((1,), (1,)), ((), ())), preferred_element_type=F32)


def f32(v):
    return v.astype(F32)


def over(ns, body):
    ns = list(ns)
    straight = ns == list(range(ns[0], ns[0] + len(ns)))
    codes = (0 if straight else sum(n * 16**i for i, n in enumerate(ns)),
             sum(STEPS[n][0] * 4**i for i, n in enumerate(ns)),
             sum(STEPS[n][1] * 4**i for i, n in enumerate(ns)))

    def one(i, carry):
        cn, cx, cy = carry
        body(ns[0] + i if straight else lax.rem(cn, 16), lax.rem(cx, 4), lax.rem(cy, 4))
        return lax.div(cn, 16), lax.div(cx, 4), lax.div(cy, 4)

    lax.fori_loop(0, len(ns), one, tuple(jnp.int32(v) for v in codes))


def kernel(mask_ref, len_ref, q_hbm, g_hbm, k_hbm, v_hbm, attv, qgv, zbuf,
           kin, vin, q, g, strips, sendbuf, kv, vo, kord, bias, s_buf, vd_buf, p_buf, m_part, m_near, m_all,
           off, acc_near, acc, qTf, gTf, qT, gT, gbuf, sbuf, bbuf, abuf, w,
           in_sem, z_send, z_recv, a_send, a_recv, b_send, b_recv, s_send, s_recv,
           rs_send, rs_recv, rb_send, rb_recv, ra_send, ra_recv, rz_send, rz_recv):
    me = Place()
    a, b, z, c = me.a, me.b, me.z, me.c
    R = q.shape[0]
    RB = 256
    sib = me.chip(z, 1 - c)
    ins = [pltpu.make_async_copy(s, d, in_sem.at[i])
           for i, (s, d) in enumerate(((k_hbm, kin), (v_hbm, vin), (q_hbm, q), (g_hbm, g)))]
    for cp in ins:
        cp.start()
    barrier = pltpu.get_barrier_semaphore()
    partners = [me.at((a + o) % 4, b) for o in (1, 2, 3)] + [me.at(a, (b + o) % 4) for o in (1, 2, 3)]
    partners += [me.chip((z + d) % NZ, (c + r) % 2) for d in range(NZ) for r in range(2) if d or r]
    for dev in partners:
        pl.semaphore_signal(barrier, inc=1, device_id=dev, device_id_type=MESH)
    ins[0].wait()
    ins[1].wait()
    for i, ref in enumerate((kin, vin)):
        strips[i] = f32(ref[...]).reshape(128, 128)
    for i in range(2):
        for h in range(NZ):
            sendbuf[i, h] = strips[i, pl.ds(h, 16, stride=8), :].astype(BF16)
    pl.semaphore_wait(barrier, len(partners))

    strip = pl.ds(pl.multiple_of(c * 16, 16), 16)
    for d in range(NZ):
        h = (z + d) % NZ
        for r in range(2):
            ct = (c + r) % 2
            src, dst = sendbuf.at[ct, h], kv.at[ct, z, me.x, me.y, strip]
            if d or r:
                rcopy(src, dst, z_send.at[r], z_recv, me.chip(h, ct)).start()
            else:
                pltpu.make_async_copy(src, dst, z_recv).start()

    ins[2].wait()
    ins[3].wait()
    comp = lax.axis_index("prefix") * (R // 8) // SPAN
    nrow = (len_ref[comp] - lax.axis_index("prefix") * (R // 8) % SPAN) * 8
    valid = lax.broadcasted_iota(jnp.int32, (R, 128), 0) < nrow
    g[...] = jnp.where(valid, f32(g[...]), 0.0).astype(BF16)
    vo[:, 128:256] = jnp.ones((vo.shape[0], 128), BF16)
    lane = lax.broadcasted_iota(jnp.int32, (8, BLK), 1) // 32
    for x in range(4):
        row = jnp.zeros((8, BLK), F32)
        for zz in range(NZ):
            t = zz * 4 + x
            if t:
                level = (1.0 - mask_ref[comp, t].astype(F32)) * HIDDEN
                row = jnp.where(lane == zz, level, row)
        bias[x] = row
    m_part[...] = jnp.full((R, 128), -jnp.inf, F32)
    qTf[...] = jnp.transpose(f32(q[...]))
    gTf[...] = jnp.transpose(f32(g[...]))

    def mirror(n):
        pair = 1 - 2 * lax.rem(n + 1, 2)
        return jnp.where((n < 3) | (n == 15), n, n + pair)

    def block(dx, dy):
        return (me.x + dx) % 4, (me.y + dy) % 4

    def at_pos(n):
        return pl.ds(pl.multiple_of(n * BLK, BLK), BLK)

    def scores_and_dots(n, dx, dy):
        x, y = block(dx, dy)
        k = kv[0, :, x, y].reshape(BLK, 128)
        kord[at_pos(n), :] = k
        x2, y2 = block(dy, dx)
        n2 = mirror(n)
        v = kv[1, :, x2, y2].reshape(BLK, 128)
        vo[at_pos(n2), 0:128] = v
        for r in range(0, R, RB):
            s = dot_nt(q[r:r + RB, :], k)
            s = (s.reshape(RB // 8, 8, BLK) + bias[x][None]).reshape(RB, BLK)
            s_buf[n, r:r + RB, :] = s
            m_part[r:r + RB, :] = jnp.maximum(m_part[r:r + RB, :], jnp.maximum(s[:, :128], s[:, 128:]))
            vd_buf[n2, r:r + RB, :] = dot_nt(g[r:r + RB, :], v)

    def weights(m_ref):
        def one(n, dx, dy):
            for r in range(0, R, RB):
                m = m_ref[r:r + RB, :]
                for j in range(2):
                    p = jnp.exp2((s_buf[n, r:r + RB, 128 * j:128 * j + 128] - m) * C2)
                    p_buf[r:r + RB, pl.ds(pl.multiple_of(n * BLK + 128 * j, 128), 128)] = p.astype(BF16)
        return one

    def top(ref):
        ref[...] = jnp.broadcast_to(jnp.max(m_part[...], axis=1, keepdims=True), (R, 128))

    sends = []

    def send(ref, ss, rs, dev):
        cp = rcopy(ref, ref, ss, rs, dev)
        cp.start()
        sends.append(cp)

    def blk(da, db):
        x, y = me.turn((a + da) % 4, (b + db) % 4)
        return kv.at[c, :, x, y]

    def hand_over(da, db):
        dx, dy = me.turn(jnp.int32(da), jnp.int32(db))
        send(blk(da, db), s_send.at[da, db], s_recv.at[dx, dy], sib)

    def handed(da, db):
        dx, dy = me.turn_other(jnp.int32(da), jnp.int32(db))
        x, y = block(dx, dy)
        wait(kv.at[1 - c, :, x, y], s_recv.at[dx, dy])

    def along_b(k):
        for i, o in enumerate(RING):
            send(blk(COLS[k], 0), b_send.at[i, k], b_recv.at[i, k], me.at(a, (b + 4 - o) % 4))
        hand_over(COLS[k], 0)

    def arrived(k):
        for i, o in enumerate(RING):
            wait(blk(COLS[k], o), b_recv.at[i, k])
            hand_over(COLS[k], o)

    wait(blk(0, 0), z_recv)
    for i, o in enumerate(RING):
        send(blk(0, 0), a_send.at[i], a_recv.at[i], me.at((a + 4 - o) % 4, b))
    along_b(0)
    for k in range(1, 4):
        wait(blk(COLS[k], 0), a_recv.at[k - 1])
        along_b(k)
    arrived(0)
    for k in range(4):
        handed(COLS[k], 0)
    for o in RING:
        handed(0, o)
    over(NEAR, scores_and_dots)
    top(m_near)
    arrived(1)
    over(NEAR, weights(m_near))
    lo = NEAR[0] * BLK
    for r in range(0, R, RB):
        acc_near[r:r + RB, :] = dot(p_buf[r:r + RB, lo:], vo[lo:, :])
    for k in range(1, 4):
        if k > 1:
            arrived(k)
        for o in RING:
            handed(COLS[k], o)
        over([n for n in FAR if STEPS[n][0] == COLS[k]], scores_and_dots)
    top(m_all)
    over(FAR, weights(m_all))
    for r in range(0, R, RB):
        rows = slice(r, r + RB)
        f = jnp.exp2((m_near[rows, :] - m_all[rows, :]) * C2)
        m_near[rows, :] = f
        part = dot(p_buf[rows, :lo], vo[:lo, :])
        total = part[:, :128] + f * acc_near[rows, :128]
        rl = 1.0 / (part[:, 128:] + f * acc_near[rows, 128:])
        mixed = jnp.where(valid[rows, :], total * rl, 0.0)
        attv[rows, :] = mixed.astype(BF16)
        off[rows, :] = jnp.broadcast_to(jnp.sum(f32(g[rows, :]) * mixed, axis=1, keepdims=True), (RB, 128))
        m_all[rows, :] = rl
        rlT = jnp.transpose(rl)
        fT = jnp.transpose(f)
        qs = qTf[:, rows] * (rlT * ROOT)
        gs = gTf[:, rows] * rlT
        qT[0, :, rows] = qs.astype(BF16)
        qT[1, :, rows] = (qs * fT).astype(BF16)
        gT[0, :, rows] = gs.astype(BF16)
        gT[1, :, rows] = (gs * fT).astype(BF16)

    def part_sum(n):
        wait(sbuf.at[n], rs_recv.at[n])
        return f32(sbuf[n]) + f32(gbuf[n, c])

    def to_b(n, dx, dy):
        da, db = me.turn(dx, dy)

        @pl.when(db != 0)
        def _():
            sbuf[n] = part_sum(n).astype(BF16)
            rcopy(sbuf.at[n], bbuf.at[db - 1, da], rb_send.at[db - 1, da], rb_recv.at[db - 1, da],
                  me.at(a, (b + db) % 4)).start()

    def gradients(n, dx, dy):
        far = lax.div(n, 9)
        cols = at_pos(n)
        kg, vg = jnp.zeros((128, BLK), F32), jnp.zeros((128, BLK), F32)
        for r in range(0, R, RB):
            rows = slice(r, r + RB)
            p = p_buf[rows, cols]
            o = jnp.concatenate([off[rows, :]] * 2, axis=1)
            ds = (f32(p) * (vd_buf[n, rows, :] - o)).astype(BF16)
            p_buf[rows, cols] = ds
            kg += dot(qT[far, :, rows], ds)
            vg += dot(gT[far, :, rows], p)
        gbuf[n, 0] = jnp.transpose(kg).astype(BF16).reshape(NZ, 32, 128)
        gbuf[n, 1] = jnp.transpose(vg).astype(BF16).reshape(NZ, 32, 128)
        rcopy(gbuf.at[n, 1 - c], sbuf.at[n], rs_send.at[n], rs_recv.at[n], sib).start()

    LAG = 2

    codes = tuple(sum(s[i] * 4**j for j, s in enumerate(STEPS)) for i in range(2))

    def one(n, carry):
        cx, cy, ox, oy = carry
        dx, dy = lax.rem(cx, 4), lax.rem(cy, 4)
        gradients(n, dx, dy)

        @pl.when(n >= LAG)
        def _():
            to_b(n - LAG, lax.rem(ox, 4), lax.rem(oy, 4))
        step = jnp.where(n >= LAG, 4, 1)
        return lax.div(cx, 4), lax.div(cy, 4), lax.div(ox, step), lax.div(oy, step)

    lax.fori_loop(0, 16, one, tuple(jnp.int32(v) for v in codes + codes))
    for n in range(16 - LAG, 15):
        to_b(n, jnp.int32(STEPS[n][0]), jnp.int32(STEPS[n][1]))

    for r in range(0, R, RB):
        rows = slice(r, r + RB)
        t = dot(p_buf[rows, :lo], kord[:lo, :]) + m_near[rows, :] * dot(p_buf[rows, lo:], kord[lo:, :])
        qgv[rows, :] = (t * (m_all[rows, :] * ROOT)).astype(BF16)

    tail = []
    for n in NEAR:
        dx, dy = STEPS[n]
        if dx and not dy:
            da = dx
            m = n + c * (STEPS.index((0, dx)) - n)
            total = part_sum(m)
            for i in range(3):
                wait(bbuf.at[i, da], rb_recv.at[i, da])
                total = total + f32(bbuf[i, da])
            sbuf[m] = total.astype(BF16)
            cp = rcopy(sbuf.at[m], abuf.at[da - 1], ra_send.at[da - 1], ra_recv.at[da - 1], me.at((a + da) % 4, b))
            cp.start()
            tail.append(cp)
    total = part_sum(15)
    for i in range(3):
        wait(bbuf.at[i, 0], rb_recv.at[i, 0])
        total = total + f32(bbuf[i, 0])
    for i in range(3):
        wait(abuf.at[i], ra_recv.at[i])
        total = total + f32(abuf[i])
    w[...] = total.astype(BF16)
    for d in range(NZ):
        t = (z + d) % NZ
        for r in range(2):
            ct = (c + r) % 2
            src, dst = w.at[t, pl.ds(pl.multiple_of(ct * 16, 16), 16)], zbuf.at[c, z]
            if d or r:
                rcopy(src, dst, rz_send.at[r], rz_recv, me.chip(t, ct)).start()
            else:
                pltpu.make_async_copy(src, dst, rz_recv).start()
    for cp in sends + tail:
        cp.wait_send()
    wait(sendbuf.at[0, pl.ds(0, 7)], z_send.at[0])
    wait(sendbuf.at[0], z_send.at[1])
    for n in range(16):
        wait(gbuf.at[n, 0], rs_send.at[n])
    for i in range(3):
        for j in range(4):
            wait(bbuf.at[i, j], rb_send.at[i, j])
    wait(zbuf, rz_recv)
    wait(zbuf.at[0, pl.ds(0, 7)], rz_send.at[0])
    wait(zbuf.at[0], rz_send.at[1])


def write_kernel(att_in, qg_in, zbuf, att, qg, kg, vg, buf, sem):
    cps = [pltpu.make_async_copy(att_in, att, sem.at[0]), pltpu.make_async_copy(qg_in, qg, sem.at[1])]
    for cp in cps:
        cp.start()
    for i, dst in enumerate((kg, vg)):
        for h in range(NZ):
            buf[i, pl.ds(h, 16, stride=8), :] = f32(zbuf[i, h])
        cps.append(pltpu.make_async_copy(buf.at[i], dst, sem.at[2 + i]))
        cps[-1].start()
    for cp in cps:
        cp.wait()


def on_device(queries, prefix_keys, prefix_values, out_grad, tile_mask, lengths):
    R = queries.shape[0] * queries.shape[1]
    S = 16 * BLK
    sm, hbm = pl.BlockSpec(memory_space=pltpu.SMEM), pl.BlockSpec(memory_space=pl.ANY)
    vmem, dma = pltpu.VMEM, pltpu.SemaphoreType.DMA
    rows = jax.ShapeDtypeStruct((R, 128), BF16)
    att, qg, heads = pl.pallas_call(
        kernel,
        out_shape=(rows, rows, jax.ShapeDtypeStruct((2, NZ, 16, 128), BF16)),
        in_specs=[sm, sm, hbm, hbm, hbm, hbm],
        out_specs=(pl.BlockSpec(memory_space=vmem),) * 3,
        scratch_shapes=[
            vmem((16, 8, 128), BF16), vmem((16, 8, 128), BF16), vmem((R, 128), BF16), vmem((R, 128), BF16),
            vmem((2, 128, 128), F32), vmem((2, NZ, 16, 128), BF16), vmem((2, NZ, 4, 4, 32, 128), BF16),
            vmem((S, 256), BF16), vmem((S, 128), BF16), vmem((4, 8, BLK), F32),
            vmem((16, R, BLK), F32), vmem((16, R, BLK), F32), vmem((R, S), BF16),
            vmem((R, 128), F32), vmem((R, 128), F32), vmem((R, 128), F32),
            vmem((R, 128), F32), vmem((R, 256), F32), vmem((8, 128), F32),
            vmem((128, R), F32), vmem((128, R), F32), vmem((2, 128, R), BF16), vmem((2, 128, R), BF16),
            vmem((16, 2, NZ, 32, 128), BF16), vmem((16, NZ, 32, 128), BF16), vmem((3, 4, NZ, 32, 128), BF16),
            vmem((3, NZ, 32, 128), BF16), vmem((NZ, 32, 128), BF16),
            dma((4,)), dma((2,)), dma, dma((3,)), dma((3,)), dma((3, 4)), dma((3, 4)),
            dma((4, 4)), dma((4, 4)), dma((16,)), dma((16,)), dma((3, 4)), dma((3, 4)), dma((3,)), dma((3,)),
            dma((2,)), dma,
        ],
        compiler_params=pltpu.CompilerParams(collective_id=0, has_side_effects=True,
                                             vmem_limit_bytes=60 * 2**20),
        name="shared_prompt",
    )(tile_mask, lengths, queries.reshape(R, 128), out_grad.reshape(R, 128), prefix_keys, prefix_values)
    grads = jax.ShapeDtypeStruct((128, 128), F32)
    att, qg, kg, vg = pl.pallas_call(
        write_kernel,
        out_shape=(rows, rows, grads, grads),
        in_specs=[pl.BlockSpec(memory_space=vmem)] * 3,
        out_specs=(hbm, hbm, hbm, hbm),
        scratch_shapes=[vmem((2, 128, 128), F32), dma((4,))],
        name="write_out",
    )(att, qg, heads)
    shape = prefix_keys.shape
    return att.reshape(queries.shape), qg.reshape(queries.shape), kg.reshape(shape), vg.reshape(shape)


def solution(mesh):
    tokens, owned = P("prefix", "group", None), P(("group", "prefix"), None, None)
    return jax.shard_map(
        on_device,
        mesh=mesh,
        in_specs=(tokens, owned, owned, tokens, P(), P()),
        out_specs=(tokens, tokens, owned, owned),
        check_vma=False,
    )
```

time: 344 us -> 64.9 us (0.19)
  waiting for transfers between devices: 225 us -> 0 us
  Pallas kernels: 0 us -> 64.1 us
  matrix products: 41.6 us -> 0 us
  local copies, waits for them, and re-layouts: 20 us -> 0 us
  starting transfers between devices: 17.2 us -> 0 us
  blocking collectives: 15.8 us -> 0 us
  between operations: 13.9 us -> 0.64 us
  other arithmetic: 8.56 us -> 0 us
    unnamed x5 -> x0, waiting for transfers between devices: 79.4 us -> none
    reduce_scatter x1 -> x0, waiting for transfers between devices: 73.1 us -> none  [on_device(): lax.psum_scatter(key_part.astype(jnp.bfloat16), 'prefix', scatter_dimensi...]
    all_gather x2 -> x0, waiting for transfers between devices: 69.5 us -> none  [the longest x1 35.6 us: on_device(): lax.all_gather(owned_values, 'prefix', axis=0, tiled=True)]
    pallas_call x0 -> x2, Pallas kernels: none -> 64.1 us  [the longest x1 62.2 us: on_device(): pl.pallas_call(kernel, out_shape=(rows, rows, jax.ShapeDtypeStruct((2, NZ...]
    dot_general x6 -> x0, matrix products: 41.6 us -> none  [the longest x1 9.22 us: on_device(): jnp.einsum('gtrs,sgd->tgrd', weights, all_values, preferred_element_type=...]
    unnamed x23 -> x0, local copies, waits for them, and re-layouts: 16.9 us -> none
    all_to_all x3 -> x0, starting transfers between devices: 16.8 us -> none  [the longest x1 6.76 us: on_device(): lax.all_to_all(value_sum.astype(jnp.bfloat16), 'group', split_axis=0, con...]
    all_to_all x1 -> x0, blocking collectives: 15.8 us -> none  [on_device(): lax.all_to_all(prefix_keys, 'group', split_axis=1, concat_axis=0, tiled=T...]
  transfers between devices with their start and end apart: 7 -> 0, of which waited for: 5 -> 0; matrix products, arithmetic and copies ran while one was open for 11% -> 0% of each run, Pallas kernels for 0% -> 0%
where the time goes in v2:
time: 64.9 us; the launch traced here: 64.7 us
  Pallas kernels  64.1 us (99%)
    pallas_call x1, Pallas kernels, on_device(): pl.pallas_call(kernel, out_shape=(rows, rows, jax.ShapeDtypeStruct((2, NZ...  62.2 us
    pallas_call x1, Pallas kernels, on_device(): pl.pallas_call(write_kernel, out_shape=(rows, rows, grads, grads), in_spe...  1.89 us

profile of v2, /device:TPU:1, one launch (start us, length us, event | category | flops | bytes accessed | tf_op | source)
XLA Modules:
  0.0 64.7 jit_solution(3610607566210513203)
XLA Ops:
  0.6 62.2 %shared_prompt.1 = (bf16[1024,128]{1,0:T(8,128)(2,1)}, bf16[1024,128]{1,0:T(8,128)(2,1)}, bf16[2,8,16,128]{3,2,1,0:T(8,128)(2,1)}) custom-call(s32[2,32]{1,0:T(2,128)} %mask_ref.1, s32[2]{0:T(128)} %len_ref.1, bf16[1024,128]{1,0:T(8,128)(2,1)} %bitcast.6, bf16[1024,128]{1,0:T(8,128)(2,1)} %bitcast.7, bf16[16,8,128]{2,1,0:T(8,128)(2,1)} %k_hbm.1, ...), custom_call_target="tpu_custom_call" | custom-call | tf_op jit(solution)/shard_map/shared_prompt/pallas_call | solution.py:374
  62.8 1.9 %write_out.1 = (bf16[1024,128]{1,0:T(8,128)(2,1)}, bf16[1024,128]{1,0:T(8,128)(2,1)}, f32[128,128]{1,0:T(8,128)}, f32[128,128]{1,0:T(8,128)}) custom-call(bf16[1024,128]{1,0:T(8,128)(2,1)} %get-tuple-element.11.att_in, bf16[1024,128]{1,0:T(8,128)(2,1)} %get-tuple-element.12.qg_in, bf16[2,8,16,128]{3,2,1,0:T(8,128)(2,1)} %get-tuple-element.13.zbuf), custom_call_target="tpu_custom_call" | custom-call | tf_op jit(solution)/shard_map/write_out/pallas_call | solution.py:398

commit v3 on v2

--- a/solution.py
+++ b/solution.py
@@ -17,7 +17,7 @@
 C2 = ROOT * math.log2(math.e)
 HIDDEN = -1e30
 
-STEPS = [(2, 2), (1, 1), (3, 3), (2, 1), (1, 2), (2, 3), (3, 2), (1, 3), (3, 1),
+STEPS = [(2, 2), (2, 1), (1, 2), (2, 3), (3, 2), (1, 1), (1, 3), (3, 1), (3, 3),
          (2, 0), (0, 2), (1, 0), (0, 1), (3, 0), (0, 3), (0, 0)]
 FAR, NEAR = range(0, 9), range(9, 16)
 RING = (3, 1, 2)
@@ -81,16 +81,31 @@
     lax.fori_loop(0, len(ns), one, tuple(jnp.int32(v) for v in codes))
 
 
+def each(ns, body):
+    for n in ns:
+        body(n, *STEPS[n])
+
+
+def pick(n, values):
+    out = jnp.int32(values[0])
+    for i, v in enumerate(values[1:], 1):
+        out = jnp.where(n == i, v, out)
+    return out
+
+
 def kernel(mask_ref, len_ref, q_hbm, g_hbm, k_hbm, v_hbm, attv, qgv, zbuf,
            kin, vin, q, g, strips, sendbuf, kv, vo, kord, bias, s_buf, vd_buf, p_buf, m_part, m_near, m_all,
-           off, acc_near, acc, qTf, gTf, qT, gT, gbuf, sbuf, bbuf, abuf, w,
-           in_sem, z_send, z_recv, a_send, a_recv, b_send, b_recv, s_send, s_recv,
-           rs_send, rs_recv, rb_send, rb_recv, ra_send, ra_recv, rz_send, rz_recv):
+           off, acc_near, qTf, gTf, qT, gT, gbuf, sbuf, bbuf, abuf, w,
+           in_sem, z_send, z_self, z_recv, a_send, a_recv, b_send, b_recv, s_send, s_recv,
+           rs_send, rs_recv, rb_send, rb_recv, ra_send, ra_recv, rz_send, rz_self, rz_recv):
     me = Place()
     a, b, z, c = me.a, me.b, me.z, me.c
     R = q.shape[0]
     RB = 256
+    K, V = 0, 1
     sib = me.chip(z, 1 - c)
+    mine, others = pl.ds(pl.multiple_of(c * 4, 4), 4), pl.ds(pl.multiple_of(4 - c * 4, 4), 4)
+    my_half = lax.div(z, 4)
     ins = [pltpu.make_async_copy(s, d, in_sem.at[i])
            for i, (s, d) in enumerate(((k_hbm, kin), (v_hbm, vin), (q_hbm, q), (g_hbm, g)))]
     for cp in ins:
@@ -100,25 +115,29 @@
     partners += [me.chip((z + d) % NZ, (c + r) % 2) for d in range(NZ) for r in range(2) if d or r]
     for dev in partners:
         pl.semaphore_signal(barrier, inc=1, device_id=dev, device_id_type=MESH)
-    ins[0].wait()
-    ins[1].wait()
     for i, ref in enumerate((kin, vin)):
+        ins[i].wait()
         strips[i] = f32(ref[...]).reshape(128, 128)
-    for i in range(2):
         for h in range(NZ):
             sendbuf[i, h] = strips[i, pl.ds(h, 16, stride=8), :].astype(BF16)
     pl.semaphore_wait(barrier, len(partners))
 
+    def to_or_keep(src, dst, ss, rs, here, dev):
+        @pl.when(here)
+        def _():
+            pltpu.make_async_copy(src, dst, rs).start()
+
+        @pl.when(jnp.logical_not(here))
+        def _():
+            rcopy(src, dst, ss, rs, dev).start()
+
     strip = pl.ds(pl.multiple_of(c * 16, 16), 16)
-    for d in range(NZ):
-        h = (z + d) % NZ
-        for r in range(2):
-            ct = (c + r) % 2
-            src, dst = sendbuf.at[ct, h], kv.at[ct, z, me.x, me.y, strip]
-            if d or r:
-                rcopy(src, dst, z_send.at[r], z_recv, me.chip(h, ct)).start()
-            else:
-                pltpu.make_async_copy(src, dst, z_recv).start()
+    for i in (K, V):
+        dst = kv.at[i, z, me.x, me.y, strip]
+        for d in range(1, NZ):
+            h = (z + d) % NZ
+            rcopy(sendbuf.at[i, h], dst, z_send.at[i], z_recv.at[i], me.chip(h, my_half)).start()
+        to_or_keep(sendbuf.at[i, z], dst, z_self.at[i], z_recv.at[i], my_half == c, sib)
 
     ins[2].wait()
     ins[3].wait()
@@ -137,33 +156,31 @@
                 row = jnp.where(lane == zz, level, row)
         bias[x] = row
     m_part[...] = jnp.full((R, 128), -jnp.inf, F32)
-    qTf[...] = jnp.transpose(f32(q[...]))
-    gTf[...] = jnp.transpose(f32(g[...]))
-
-    def mirror(n):
-        pair = 1 - 2 * lax.rem(n + 1, 2)
-        return jnp.where((n < 3) | (n == 15), n, n + pair)
 
     def block(dx, dy):
         return (me.x + dx) % 4, (me.y + dy) % 4
 
     def at_pos(n):
-        return pl.ds(pl.multiple_of(n * BLK, BLK), BLK)
-
-    def scores_and_dots(n, dx, dy):
+        return pl.ds(n * BLK if isinstance(n, int) else pl.multiple_of(n * BLK, BLK), BLK)
+
+    def scores(n, dx, dy):
         x, y = block(dx, dy)
-        k = kv[0, :, x, y].reshape(BLK, 128)
+        k = kv[K, :, x, y].reshape(BLK, 128)
         kord[at_pos(n), :] = k
-        x2, y2 = block(dy, dx)
-        n2 = mirror(n)
-        v = kv[1, :, x2, y2].reshape(BLK, 128)
-        vo[at_pos(n2), 0:128] = v
         for r in range(0, R, RB):
             s = dot_nt(q[r:r + RB, :], k)
             s = (s.reshape(RB // 8, 8, BLK) + bias[x][None]).reshape(RB, BLK)
             s_buf[n, r:r + RB, :] = s
             m_part[r:r + RB, :] = jnp.maximum(m_part[r:r + RB, :], jnp.maximum(s[:, :128], s[:, 128:]))
-            vd_buf[n2, r:r + RB, :] = dot_nt(g[r:r + RB, :], v)
+
+    def values_in(n, dx, dy):
+        x, y = block(dx, dy)
+        vo[at_pos(n), 0:128] = kv[V, :, x, y].reshape(BLK, 128)
+
+    def value_dots(n, dx, dy):
+        v = vo[at_pos(n), 0:128]
+        for r in range(0, R, RB):
+            vd_buf[n, r:r + RB, :] = dot_nt(g[r:r + RB, :], v)
 
     def weights(m_ref):
         def one(n, dx, dy):
@@ -184,56 +201,78 @@
         cp.start()
         sends.append(cp)
 
-    def blk(da, db):
+    def blk(i, da, db):
         x, y = me.turn((a + da) % 4, (b + db) % 4)
-        return kv.at[c, :, x, y]
-
-    def hand_over(da, db):
+        return kv.at[i, mine, x, y]
+
+    def hand_over(i, da, db):
         dx, dy = me.turn(jnp.int32(da), jnp.int32(db))
-        send(blk(da, db), s_send.at[da, db], s_recv.at[dx, dy], sib)
-
-    def handed(da, db):
+        send(blk(i, da, db), s_send.at[i, da, db], s_recv.at[i, dx, dy], sib)
+
+    def handed(i, da, db):
         dx, dy = me.turn_other(jnp.int32(da), jnp.int32(db))
         x, y = block(dx, dy)
-        wait(kv.at[1 - c, :, x, y], s_recv.at[dx, dy])
-
-    def along_b(k):
-        for i, o in enumerate(RING):
-            send(blk(COLS[k], 0), b_send.at[i, k], b_recv.at[i, k], me.at(a, (b + 4 - o) % 4))
-        hand_over(COLS[k], 0)
-
-    def arrived(k):
-        for i, o in enumerate(RING):
-            wait(blk(COLS[k], o), b_recv.at[i, k])
-            hand_over(COLS[k], o)
-
-    wait(blk(0, 0), z_recv)
-    for i, o in enumerate(RING):
-        send(blk(0, 0), a_send.at[i], a_recv.at[i], me.at((a + 4 - o) % 4, b))
-    along_b(0)
-    for k in range(1, 4):
-        wait(blk(COLS[k], 0), a_recv.at[k - 1])
-        along_b(k)
-    arrived(0)
-    for k in range(4):
-        handed(COLS[k], 0)
-    for o in RING:
-        handed(0, o)
-    over(NEAR, scores_and_dots)
+        wait(kv.at[i, others, x, y], s_recv.at[i, dx, dy])
+
+    def along_b(i, k):
+        for j, o in enumerate(RING):
+            send(blk(i, COLS[k], 0), b_send.at[i, j, k], b_recv.at[i, j, k], me.at(a, (b + 4 - o) % 4))
+        hand_over(i, COLS[k], 0)
+
+    def arrived(i, k):
+        for j, o in enumerate(RING):
+            wait(blk(i, COLS[k], o), b_recv.at[i, j, k])
+            hand_over(i, COLS[k], o)
+
+    def handed_far(i, k):
+        for o in RING:
+            handed(i, COLS[k], o)
+
+    def handed_near(i):
+        for k in range(4):
+            handed(i, COLS[k], 0)
+        handed_far(i, 0)
+
+    for i in (K, V):
+        wait(blk(i, 0, 0), z_recv.at[i])
+        for j, o in enumerate(RING):
+            send(blk(i, 0, 0), a_send.at[i, j], a_recv.at[i, j], me.at((a + 4 - o) % 4, b))
+        along_b(i, 0)
+    qTf[...] = jnp.transpose(f32(q[...]))
+    gTf[...] = jnp.transpose(f32(g[...]))
+    for i in (K, V):
+        for k in range(1, 4):
+            wait(blk(i, COLS[k], 0), a_recv.at[i, k - 1])
+            along_b(i, k)
+    arrived(K, 0)
+    handed_near(K)
+    each(NEAR, scores)
+    arrived(V, 0)
     top(m_near)
-    arrived(1)
     over(NEAR, weights(m_near))
+    arrived(K, 1)
+    arrived(K, 2)
+    handed_near(V)
+    over(NEAR, values_in)
     lo = NEAR[0] * BLK
     for r in range(0, R, RB):
         acc_near[r:r + RB, :] = dot(p_buf[r:r + RB, lo:], vo[lo:, :])
-    for k in range(1, 4):
-        if k > 1:
-            arrived(k)
-        for o in RING:
-            handed(COLS[k], o)
-        over([n for n in FAR if STEPS[n][0] == COLS[k]], scores_and_dots)
+    each(NEAR, value_dots)
+    arrived(K, 3)
+    handed_far(K, 1)
+    handed_far(K, 2)
+    each(range(5, 9), scores)
+    arrived(V, 1)
+    handed_far(K, 3)
+    each(range(5), scores)
+    arrived(V, 2)
     top(m_all)
     over(FAR, weights(m_all))
+    arrived(V, 3)
+    for k in range(1, 4):
+        handed_far(V, k)
+    over(FAR, values_in)
+    each(FAR, value_dots)
     for r in range(0, R, RB):
         rows = slice(r, r + RB)
         f = jnp.exp2((m_near[rows, :] - m_all[rows, :]) * C2)
@@ -256,10 +295,13 @@
 
     def part_sum(n):
         wait(sbuf.at[n], rs_recv.at[n])
-        return f32(sbuf[n]) + f32(gbuf[n, c])
-
-    def to_b(n, dx, dy):
-        da, db = me.turn(dx, dy)
+        return f32(sbuf[n]) + f32(gbuf[n, :, mine])
+
+    def to_b(n):
+        if isinstance(n, int):
+            da, db = me.turn(jnp.int32(STEPS[n][0]), jnp.int32(STEPS[n][1]))
+        else:
+            da, db = me.turn(pick(n, [s[0] for s in STEPS]), pick(n, [s[1] for s in STEPS]))
 
         @pl.when(db != 0)
         def _():
@@ -267,8 +309,7 @@
             rcopy(sbuf.at[n], bbuf.at[db - 1, da], rb_send.at[db - 1, da], rb_recv.at[db - 1, da],
                   me.at(a, (b + db) % 4)).start()
 
-    def gradients(n, dx, dy):
-        far = lax.div(n, 9)
+    def gradients(n, far):
         cols = at_pos(n)
         kg, vg = jnp.zeros((128, BLK), F32), jnp.zeros((128, BLK), F32)
         for r in range(0, R, RB):
@@ -279,77 +320,86 @@
             p_buf[rows, cols] = ds
             kg += dot(qT[far, :, rows], ds)
             vg += dot(gT[far, :, rows], p)
-        gbuf[n, 0] = jnp.transpose(kg).astype(BF16).reshape(NZ, 32, 128)
-        gbuf[n, 1] = jnp.transpose(vg).astype(BF16).reshape(NZ, 32, 128)
-        rcopy(gbuf.at[n, 1 - c], sbuf.at[n], rs_send.at[n], rs_recv.at[n], sib).start()
-
-    LAG = 2
-
-    codes = tuple(sum(s[i] * 4**j for j, s in enumerate(STEPS)) for i in range(2))
-
-    def one(n, carry):
-        cx, cy, ox, oy = carry
-        dx, dy = lax.rem(cx, 4), lax.rem(cy, 4)
-        gradients(n, dx, dy)
-
-        @pl.when(n >= LAG)
+        gbuf[n, K] = jnp.transpose(kg).astype(BF16).reshape(NZ, 32, 128)
+        gbuf[n, V] = jnp.transpose(vg).astype(BF16).reshape(NZ, 32, 128)
+
+    def to_sibling(n):
+        rcopy(gbuf.at[n, :, others], sbuf.at[n], rs_send.at[n], rs_recv.at[n], sib).start()
+
+    def three(i, _):
+        for j in range(3):
+            gradients(3 * i + j, 0)
+        for j in range(3):
+            to_sibling(3 * i + j)
+
+        @pl.when(i > 0)
         def _():
-            to_b(n - LAG, lax.rem(ox, 4), lax.rem(oy, 4))
-        step = jnp.where(n >= LAG, 4, 1)
-        return lax.div(cx, 4), lax.div(cy, 4), lax.div(ox, step), lax.div(oy, step)
-
-    lax.fori_loop(0, 16, one, tuple(jnp.int32(v) for v in codes + codes))
-    for n in range(16 - LAG, 15):
-        to_b(n, jnp.int32(STEPS[n][0]), jnp.int32(STEPS[n][1]))
-
+            for j in range(3):
+                to_b(3 * i + j - 3)
+        return 0
+
+    lax.fori_loop(0, 3, three, 0)
+    for now, before in ((NEAR[:4], FAR[6:]), (NEAR[4:], NEAR[:4]), ((), (13, 14))):
+        for n in now:
+            gradients(n, 1)
+        for n in now:
+            to_sibling(n)
+        for n in before:
+            to_b(n)
+
+    tail = []
+    for n in NEAR:
+        da, dy = STEPS[n]
+        if da and not dy:
+            m = n + c * (STEPS.index((0, da)) - n)
+            total = part_sum(m)
+            for j in range(3):
+                wait(bbuf.at[j, da], rb_recv.at[j, da])
+                total = total + f32(bbuf[j, da])
+            sbuf[m] = total.astype(BF16)
+            cp = rcopy(sbuf.at[m], abuf.at[da - 1], ra_send.at[da - 1], ra_recv.at[da - 1], me.at((a + da) % 4, b))
+            cp.start()
+            tail.append(cp)
     for r in range(0, R, RB):
         rows = slice(r, r + RB)
         t = dot(p_buf[rows, :lo], kord[:lo, :]) + m_near[rows, :] * dot(p_buf[rows, lo:], kord[lo:, :])
         qgv[rows, :] = (t * (m_all[rows, :] * ROOT)).astype(BF16)
-
-    tail = []
-    for n in NEAR:
-        dx, dy = STEPS[n]
-        if dx and not dy:
-            da = dx
-            m = n + c * (STEPS.index((0, dx)) - n)
-            total = part_sum(m)
-            for i in range(3):
-                wait(bbuf.at[i, da], rb_recv.at[i, da])
-                total = total + f32(bbuf[i, da])
-            sbuf[m] = total.astype(BF16)
-            cp = rcopy(sbuf.at[m], abuf.at[da - 1], ra_send.at[da - 1], ra_recv.at[da - 1], me.at((a + da) % 4, b))
-            cp.start()
-            tail.append(cp)
     total = part_sum(15)
-    for i in range(3):
-        wait(bbuf.at[i, 0], rb_recv.at[i, 0])
-        total = total + f32(bbuf[i, 0])
-    for i in range(3):
-        wait(abuf.at[i], ra_recv.at[i])
-        total = total + f32(abuf[i])
+    for j in range(3):
+        wait(bbuf.at[j, 0], rb_recv.at[j, 0])
+        total = total + f32(bbuf[j, 0])
+    for j in range(3):
+        wait(abuf.at[j], ra_recv.at[j])
+        total = total + f32(abuf[j])
     w[...] = total.astype(BF16)
-    for d in range(NZ):
-        t = (z + d) % NZ
+    for d in (2, 1, 3, 0):
+        t = lax.rem(z + d, 4)
         for r in range(2):
             ct = (c + r) % 2
-            src, dst = w.at[t, pl.ds(pl.multiple_of(ct * 16, 16), 16)], zbuf.at[c, z]
+            src, dst = w.at[:, t, pl.ds(pl.multiple_of(ct * 16, 16), 16)], zbuf.at[:, z]
             if d or r:
-                rcopy(src, dst, rz_send.at[r], rz_recv, me.chip(t, ct)).start()
+                rcopy(src, dst, rz_send, rz_recv, me.chip(c * 4 + t, ct)).start()
             else:
-                pltpu.make_async_copy(src, dst, rz_recv).start()
+                to_or_keep(src, dst, rz_self, rz_recv, my_half == c, me.chip(c * 4 + t, ct))
     for cp in sends + tail:
         cp.wait_send()
-    wait(sendbuf.at[0, pl.ds(0, 7)], z_send.at[0])
-    wait(sendbuf.at[0], z_send.at[1])
+    for i in (K, V):
+        wait(sendbuf.at[i, pl.ds(0, 7)], z_send.at[i])
+
+        @pl.when(my_half != c)
+        def _():
+            wait(sendbuf.at[i, 0], z_self.at[i])
     for n in range(16):
-        wait(gbuf.at[n, 0], rs_send.at[n])
-    for i in range(3):
-        for j in range(4):
-            wait(bbuf.at[i, j], rb_send.at[i, j])
+        wait(sbuf.at[n], rs_send.at[n])
+    for j in range(3):
+        for k in range(4):
+            wait(bbuf.at[j, k], rb_send.at[j, k])
+    wait(zbuf.at[:, pl.ds(0, 7)], rz_send)
+
+    @pl.when(my_half != c)
+    def _():
+        wait(zbuf.at[:, 0], rz_self)
     wait(zbuf, rz_recv)
-    wait(zbuf.at[0, pl.ds(0, 7)], rz_send.at[0])
-    wait(zbuf.at[0], rz_send.at[1])
 
 
 def write_kernel(att_in, qg_in, zbuf, att, qg, kg, vg, buf, sem):
@@ -382,13 +432,13 @@
             vmem((S, 256), BF16), vmem((S, 128), BF16), vmem((4, 8, BLK), F32),
             vmem((16, R, BLK), F32), vmem((16, R, BLK), F32), vmem((R, S), BF16),
             vmem((R, 128), F32), vmem((R, 128), F32), vmem((R, 128), F32),
-            vmem((R, 128), F32), vmem((R, 256), F32), vmem((8, 128), F32),
+            vmem((R, 128), F32), vmem((R, 256), F32),
             vmem((128, R), F32), vmem((128, R), F32), vmem((2, 128, R), BF16), vmem((2, 128, R), BF16),
-            vmem((16, 2, NZ, 32, 128), BF16), vmem((16, NZ, 32, 128), BF16), vmem((3, 4, NZ, 32, 128), BF16),
-            vmem((3, NZ, 32, 128), BF16), vmem((NZ, 32, 128), BF16),
-            dma((4,)), dma((2,)), dma, dma((3,)), dma((3,)), dma((3, 4)), dma((3, 4)),
-            dma((4, 4)), dma((4, 4)), dma((16,)), dma((16,)), dma((3, 4)), dma((3, 4)), dma((3,)), dma((3,)),
-            dma((2,)), dma,
+            vmem((16, 2, NZ, 32, 128), BF16), vmem((16, 2, 4, 32, 128), BF16), vmem((3, 4, 2, 4, 32, 128), BF16),
+            vmem((3, 2, 4, 32, 128), BF16), vmem((2, 4, 32, 128), BF16),
+            dma((4,)), dma((2,)), dma((2,)), dma((2,)), dma((2, 3)), dma((2, 3)), dma((2, 3, 4)), dma((2, 3, 4)),
+            dma((2, 4, 4)), dma((2, 4, 4)), dma((16,)), dma((16,)), dma((3, 4)), dma((3, 4)),
+            dma((3,)), dma((3,)), dma, dma, dma,
         ],
         compiler_params=pltpu.CompilerParams(collective_id=0, has_side_effects=True,
                                              vmem_limit_bytes=60 * 2**20),

time: 64.9 us -> 59.8 us (0.921)
  Pallas kernels: 64.1 us -> 58.9 us
    pallas_call x1, Pallas kernels: 62.2 us -> 57 us  [on_device(): pl.pallas_call(kernel, out_shape=(rows, rows, jax.ShapeDtypeStruct((2, NZ...]
where the time goes in v3:
time: 59.8 us; the launch traced here: 59.7 us
  Pallas kernels  58.9 us (98%)
  between operations  0.8 us (1%)
    pallas_call x1, Pallas kernels, on_device(): pl.pallas_call(kernel, out_shape=(rows, rows, jax.ShapeDtypeStruct((2, NZ...  57 us
    pallas_call x1, Pallas kernels, on_device(): pl.pallas_call(write_kernel, out_shape=(rows, rows, grads, grads), in_spe...  1.89 us

profile of v3, /device:TPU:1, one launch (start us, length us, event | category | flops | bytes accessed | tf_op | source)
XLA Modules:
  0.0 59.7 jit_solution(13574836904396659526)
XLA Ops:
  0.6 57.0 %shared_prompt.1 = (bf16[1024,128]{1,0:T(8,128)(2,1)}, bf16[1024,128]{1,0:T(8,128)(2,1)}, bf16[2,8,16,128]{3,2,1,0:T(8,128)(2,1)}) custom-call(s32[2,32]{1,0:T(2,128)} %mask_ref.1, s32[2]{0:T(128)} %len_ref.1, bf16[1024,128]{1,0:T(8,128)(2,1)} %bitcast.6, bf16[1024,128]{1,0:T(8,128)(2,1)} %bitcast.7, bf16[16,8,128]{2,1,0:T(8,128)(2,1)} %k_hbm.1, ...), custom_call_target="tpu_custom_call" | custom-call | tf_op jit(solution)/shard_map/shared_prompt/pallas_call | solution.py:424
  57.6 1.9 %write_out.1 = (bf16[1024,128]{1,0:T(8,128)(2,1)}, bf16[1024,128]{1,0:T(8,128)(2,1)}, f32[128,128]{1,0:T(8,128)}, f32[128,128]{1,0:T(8,128)}) custom-call(bf16[1024,128]{1,0:T(8,128)(2,1)} %get-tuple-element.11.att_in, bf16[1024,128]{1,0:T(8,128)(2,1)} %get-tuple-element.12.qg_in, bf16[2,8,16,128]{3,2,1,0:T(8,128)(2,1)} %get-tuple-element.13.zbuf), custom_call_target="tpu_custom_call" | custom-call | tf_op jit(solution)/shard_map/write_out/pallas_call | solution.py:448

commit v4 on v3

--- a/solution.py
+++ b/solution.py
@@ -133,8 +133,8 @@
 
     strip = pl.ds(pl.multiple_of(c * 16, 16), 16)
     for i in (K, V):
-        dst = kv.at[i, z, me.x, me.y, strip]
-        for d in range(1, NZ):
+        dst = kv.at[i, me.x, me.y, z, strip]
+        for d in (4, 3, 5, 2, 6, 1, 7):
             h = (z + d) % NZ
             rcopy(sendbuf.at[i, h], dst, z_send.at[i], z_recv.at[i], me.chip(h, my_half)).start()
         to_or_keep(sendbuf.at[i, z], dst, z_self.at[i], z_recv.at[i], my_half == c, sib)
@@ -165,7 +165,7 @@
 
     def scores(n, dx, dy):
         x, y = block(dx, dy)
-        k = kv[K, :, x, y].reshape(BLK, 128)
+        k = kv[K, x, y].reshape(BLK, 128)
         kord[at_pos(n), :] = k
         for r in range(0, R, RB):
             s = dot_nt(q[r:r + RB, :], k)
@@ -175,7 +175,7 @@
 
     def values_in(n, dx, dy):
         x, y = block(dx, dy)
-        vo[at_pos(n), 0:128] = kv[V, :, x, y].reshape(BLK, 128)
+        vo[at_pos(n), 0:128] = kv[V, x, y].reshape(BLK, 128)
 
     def value_dots(n, dx, dy):
         v = vo[at_pos(n), 0:128]
@@ -203,7 +203,7 @@
 
     def blk(i, da, db):
         x, y = me.turn((a + da) % 4, (b + db) % 4)
-        return kv.at[i, mine, x, y]
+        return kv.at[i, x, y, mine]
 
     def hand_over(i, da, db):
         dx, dy = me.turn(jnp.int32(da), jnp.int32(db))
@@ -212,10 +212,10 @@
     def handed(i, da, db):
         dx, dy = me.turn_other(jnp.int32(da), jnp.int32(db))
         x, y = block(dx, dy)
-        wait(kv.at[i, others, x, y], s_recv.at[i, dx, dy])
+        wait(kv.at[i, x, y, others], s_recv.at[i, dx, dy])
 
     def along_b(i, k):
-        for j, o in enumerate(RING):
+        for j, o in ((2, 2), (0, 3), (1, 1)):
             send(blk(i, COLS[k], 0), b_send.at[i, j, k], b_recv.at[i, j, k], me.at(a, (b + 4 - o) % 4))
         hand_over(i, COLS[k], 0)
 
@@ -235,7 +235,7 @@
 
     for i in (K, V):
         wait(blk(i, 0, 0), z_recv.at[i])
-        for j, o in enumerate(RING):
+        for j, o in ((2, 2), (0, 3), (1, 1)):
             send(blk(i, 0, 0), a_send.at[i, j], a_recv.at[i, j], me.at((a + 4 - o) % 4, b))
         along_b(i, 0)
     qTf[...] = jnp.transpose(f32(q[...]))
@@ -262,17 +262,21 @@
     handed_far(K, 1)
     handed_far(K, 2)
     each(range(5, 9), scores)
-    arrived(V, 1)
     handed_far(K, 3)
     each(range(5), scores)
+    top(m_all)
+    arrived(V, 1)
+    over(range(5), weights(m_all))
     arrived(V, 2)
-    top(m_all)
-    over(FAR, weights(m_all))
+    over(range(5, 9), weights(m_all))
     arrived(V, 3)
-    for k in range(1, 4):
-        handed_far(V, k)
-    over(FAR, values_in)
-    each(FAR, value_dots)
+    handed_far(V, 1)
+    handed_far(V, 2)
+    over(range(5, 9), values_in)
+    each(range(5, 9), value_dots)
+    handed_far(V, 3)
+    over(range(5), values_in)
+    each(range(5), value_dots)
     for r in range(0, R, RB):
         rows = slice(r, r + RB)
         f = jnp.exp2((m_near[rows, :] - m_all[rows, :]) * C2)
@@ -428,7 +432,7 @@
         out_specs=(pl.BlockSpec(memory_space=vmem),) * 3,
         scratch_shapes=[
             vmem((16, 8, 128), BF16), vmem((16, 8, 128), BF16), vmem((R, 128), BF16), vmem((R, 128), BF16),
-            vmem((2, 128, 128), F32), vmem((2, NZ, 16, 128), BF16), vmem((2, NZ, 4, 4, 32, 128), BF16),
+            vmem((2, 128, 128), F32), vmem((2, NZ, 16, 128), BF16), vmem((2, 4, 4, NZ, 32, 128), BF16),
             vmem((S, 256), BF16), vmem((S, 128), BF16), vmem((4, 8, BLK), F32),
             vmem((16, R, BLK), F32), vmem((16, R, BLK), F32), vmem((R, S), BF16),
             vmem((R, 128), F32), vmem((R, 128), F32), vmem((R, 128), F32),

time: 59.8 us -> 58.5 us (0.978)
  Pallas kernels: 58.9 us -> 57.6 us
    pallas_call x1, Pallas kernels: 57 us -> 55.7 us  [on_device(): pl.pallas_call(kernel, out_shape=(rows, rows, jax.ShapeDtypeStruct((2, NZ...]
where the time goes in v4:
time: 58.5 us; the launch traced here: 58.4 us
  Pallas kernels  57.6 us (98%)
  between operations  0.8 us (1%)
    pallas_call x1, Pallas kernels, on_device(): pl.pallas_call(kernel, out_shape=(rows, rows, jax.ShapeDtypeStruct((2, NZ...  55.7 us
    pallas_call x1, Pallas kernels, on_device(): pl.pallas_call(write_kernel, out_shape=(rows, rows, grads, grads), in_spe...  1.89 us

profile of v4, /device:TPU:1, one launch (start us, length us, event | category | flops | bytes accessed | tf_op | source)
XLA Modules:
  0.0 58.4 jit_solution(4710503050394459854)
XLA Ops:
  0.6 55.7 %shared_prompt.1 = (bf16[1024,128]{1,0:T(8,128)(2,1)}, bf16[1024,128]{1,0:T(8,128)(2,1)}, bf16[2,8,16,128]{3,2,1,0:T(8,128)(2,1)}) custom-call(s32[2,32]{1,0:T(2,128)} %mask_ref.1, s32[2]{0:T(128)} %len_ref.1, bf16[1024,128]{1,0:T(8,128)(2,1)} %bitcast.6, bf16[1024,128]{1,0:T(8,128)(2,1)} %bitcast.7, bf16[16,8,128]{2,1,0:T(8,128)(2,1)} %k_hbm.1, ...), custom_call_target="tpu_custom_call" | custom-call | tf_op jit(solution)/shard_map/shared_prompt/pallas_call | solution.py:428
  56.3 1.9 %write_out.1 = (bf16[1024,128]{1,0:T(8,128)(2,1)}, bf16[1024,128]{1,0:T(8,128)(2,1)}, f32[128,128]{1,0:T(8,128)}, f32[128,128]{1,0:T(8,128)}) custom-call(bf16[1024,128]{1,0:T(8,128)(2,1)} %get-tuple-element.11.att_in, bf16[1024,128]{1,0:T(8,128)(2,1)} %get-tuple-element.12.qg_in, bf16[2,8,16,128]{3,2,1,0:T(8,128)(2,1)} %get-tuple-element.13.zbuf), custom_call_target="tpu_custom_call" | custom-call | tf_op jit(solution)/shard_map/write_out/pallas_call | solution.py:452

commit v5 on v4

--- a/solution.py
+++ b/solution.py
@@ -93,8 +93,8 @@
     return out
 
 
-def kernel(mask_ref, len_ref, q_hbm, g_hbm, k_hbm, v_hbm, attv, qgv, zbuf,
-           kin, vin, q, g, strips, sendbuf, kv, vo, kord, bias, s_buf, vd_buf, p_buf, m_part, m_near, m_all,
+def kernel(mask_ref, len_ref, q_hbm, g_hbm, k_hbm, v_hbm, att_hbm, qg_hbm, zbuf,
+           attv, qgv, out_sem, kin, vin, q, g, strips, sendbuf, kv, vo, kord, bias, s_buf, vd_buf, p_buf, m_part, m_near, m_all,
            off, acc_near, qTf, gTf, qT, gT, gbuf, sbuf, bbuf, abuf, w,
            in_sem, z_send, z_self, z_recv, a_send, a_recv, b_send, b_recv, s_send, s_recv,
            rs_send, rs_recv, rb_send, rb_recv, ra_send, ra_recv, rz_send, rz_self, rz_recv):
@@ -276,7 +276,7 @@
     each(range(5, 9), value_dots)
     handed_far(V, 3)
     over(range(5), values_in)
-    each(range(5), value_dots)
+    each(range(3), value_dots)
     for r in range(0, R, RB):
         rows = slice(r, r + RB)
         f = jnp.exp2((m_near[rows, :] - m_all[rows, :]) * C2)
@@ -297,6 +297,9 @@
         gT[0, :, rows] = gs.astype(BF16)
         gT[1, :, rows] = (gs * fT).astype(BF16)
 
+    att_out = pltpu.make_async_copy(attv, att_hbm, out_sem.at[0])
+    att_out.start()
+
     def part_sum(n):
         wait(sbuf.at[n], rs_recv.at[n])
         return f32(sbuf[n]) + f32(gbuf[n, :, mine])
@@ -335,6 +338,10 @@
             gradients(3 * i + j, 0)
         for j in range(3):
             to_sibling(3 * i + j)
+
+        @pl.when(i == 0)
+        def _():
+            each((3, 4), value_dots)
 
         @pl.when(i > 0)
         def _():
@@ -368,6 +375,8 @@
         rows = slice(r, r + RB)
         t = dot(p_buf[rows, :lo], kord[:lo, :]) + m_near[rows, :] * dot(p_buf[rows, lo:], kord[lo:, :])
         qgv[rows, :] = (t * (m_all[rows, :] * ROOT)).astype(BF16)
+    qg_out = pltpu.make_async_copy(qgv, qg_hbm, out_sem.at[1])
+    qg_out.start()
     total = part_sum(15)
     for j in range(3):
         wait(bbuf.at[j, 0], rb_recv.at[j, 0])
@@ -403,6 +412,8 @@
     @pl.when(my_half != c)
     def _():
         wait(zbuf.at[:, 0], rz_self)
+    att_out.wait()
+    qg_out.wait()
     wait(zbuf, rz_recv)
 
 
@@ -429,8 +440,9 @@
         kernel,
         out_shape=(rows, rows, jax.ShapeDtypeStruct((2, NZ, 16, 128), BF16)),
         in_specs=[sm, sm, hbm, hbm, hbm, hbm],
-        out_specs=(pl.BlockSpec(memory_space=vmem),) * 3,
+        out_specs=(hbm, hbm, pl.BlockSpec(memory_space=vmem)),
         scratch_shapes=[
+            vmem((R, 128), BF16), vmem((R, 128), BF16), dma((2,)),
             vmem((16, 8, 128), BF16), vmem((16, 8, 128), BF16), vmem((R, 128), BF16), vmem((R, 128), BF16),
             vmem((2, 128, 128), F32), vmem((2, NZ, 16, 128), BF16), vmem((2, 4, 4, NZ, 32, 128), BF16),
             vmem((S, 256), BF16), vmem((S, 128), BF16), vmem((4, 8, BLK), F32),

time: 58.5 us -> 57.9 us (0.990)
  Pallas kernels: 57.6 us -> 56.9 us
    pallas_call x1, Pallas kernels: 55.7 us -> 55 us  [on_device(): pl.pallas_call(kernel, out_shape=(rows, rows, jax.ShapeDtypeStruct((2, NZ...]
where the time goes in v5:
time: 57.9 us; the launch traced here: 57.7 us
  Pallas kernels  56.9 us (98%)
  between operations  0.8 us (1%)
    pallas_call x1, Pallas kernels, on_device(): pl.pallas_call(kernel, out_shape=(rows, rows, jax.ShapeDtypeStruct((2, NZ...  55 us
    pallas_call x1, Pallas kernels, on_device(): pl.pallas_call(write_kernel, out_shape=(rows, rows, grads, grads), in_spe...  1.89 us

profile of v5, /device:TPU:1, one launch (start us, length us, event | category | flops | bytes accessed | tf_op | source)
XLA Modules:
  0.0 57.7 jit_solution(15308065780071438789)
XLA Ops:
  0.6 55.0 %shared_prompt.1 = (bf16[1024,128]{1,0:T(8,128)(2,1)}, bf16[1024,128]{1,0:T(8,128)(2,1)}, bf16[2,8,16,128]{3,2,1,0:T(8,128)(2,1)}) custom-call(s32[2,32]{1,0:T(2,128)} %mask_ref.1, s32[2]{0:T(128)} %len_ref.1, bf16[1024,128]{1,0:T(8,128)(2,1)} %bitcast.6, bf16[1024,128]{1,0:T(8,128)(2,1)} %bitcast.7, bf16[16,8,128]{2,1,0:T(8,128)(2,1)} %k_hbm.1, ...), custom_call_target="tpu_custom_call" | custom-call | tf_op jit(solution)/shard_map/shared_prompt/pallas_call | solution.py:439
  55.7 1.9 %write_out.1 = (bf16[1024,128]{1,0:T(8,128)(2,1)}, bf16[1024,128]{1,0:T(8,128)(2,1)}, f32[128,128]{1,0:T(8,128)}, f32[128,128]{1,0:T(8,128)}) custom-call(bf16[1024,128]{1,0:T(8,128)(2,1)} %get-tuple-element.11.att_in, bf16[1024,128]{1,0:T(8,128)(2,1)} %get-tuple-element.12.qg_in, bf16[2,8,16,128]{3,2,1,0:T(8,128)(2,1)} %get-tuple-element.13.zbuf), custom_call_target="tpu_custom_call" | custom-call | tf_op jit(solution)/shard_map/write_out/pallas_call | solution.py:464
